TPU v7x, 32 devices: a whole 2x2x4 slice. The times are simulated.
32 devices in a mesh: tx: 4 (over x, core), ty: 8 (over z, y).
Axes of the slice: x: 2, y: 2, z: 4, core: 2. Of those that a mesh axis runs over, the one named last changes fastest.
Arguments:
- granule_blocks: bfloat16 [2048, 13, 16, 128], P(('tx', 'ty')), may hold values from -6 to 6
- row_weights: bfloat16 [2048, 8, 16], P(('tx', 'ty')), may hold values from -1.5 to 1.5
- column_bank: bfloat16 [8, 128, 128], replicated, may hold values from -0.5 to 0.5
- destination: int32 [2048], P(('tx', 'ty')), may hold values from 0 to 31, as said below
- window_index: int32 [2048], P(('tx', 'ty')), may hold values from 0 to 31
- bank_index: int32 [2048], P(('tx', 'ty')), may hold values from 0 to 7
- kernel_one: bfloat16 [3, 3, 13, 64], replicated, may hold values from -1 to 1
- reduce_two: bfloat16 [2, 2, 64, 128], replicated, may hold values from -0.5 to 0.5
- kernel_two: bfloat16 [3, 3, 128, 128], replicated, may hold values from -0.25 to 0.25
- reduce_three: bfloat16 [2, 2, 128, 256], replicated, may hold values from -0.375 to 0.375
- kernel_three: bfloat16 [3, 3, 256, 256], replicated, may hold values from -0.1875 to 0.1875
- reduce_four: bfloat16 [2, 2, 256, 512], replicated, may hold values from -0.25 to 0.25
- kernel_four: bfloat16 [3, 3, 512, 512], replicated, may hold values from -0.125 to 0.125
Outputs:
- gridded: bfloat16 [13, 2048, 512], P(None, 'ty', 'tx')
- bottleneck: bfloat16 [512, 256, 64], P(None, 'ty', 'tx')
Inputs may be any that keep to these rules, and one draw needn't show every extreme that they name: At most 2 of the blocks that one device holds name the same destination; in every draw one destination is named by 2 blocks of every device.
All inputs are finite; a program needn't handle non-finite values.
Results may differ from a plain program's by a relative error of at most 0.015.
Values may be sent and summed in bfloat16 or wider, within the bound.
No kernel may reach another device: no remote copies, remote signals or barrier semaphores. Data moves between devices by JAX's collectives and lax.ppermute only.
A program may use at most 128 MiB of HBM per device.

v0:
```python
import functools

import jax
import jax.numpy as jnp
import numpy as np
from jax import lax
from jax.experimental import pallas as pl
from jax.experimental.pallas import tpu as pltpu
from jax.sharding import PartitionSpec as P

BF16 = jnp.bfloat16
F32 = jnp.float32
BANDS = 13
SRC_ROWS = 16
WIN_ROWS = 8
CAP = 2
NWIN = 32
TILE_COLS = 128
LINES = BANDS * WIN_ROWS
PACKED = CAP * LINES + WIN_ROWS
STEP_BLOCKS = 16
PIECES = 4
PHASES = 8
SPOTS = TILE_COLS // PHASES
HALO = 2
WIDE = SPOTS + 2 * HALO
TALL = NWIN + 2 * HALO
POINTS = WIDE * TALL
GROUP = 4
GROUP_POINTS = GROUP * WIDE
MARGIN = 24
MIB = 1024 * 1024


def dot(a, b):
    return jnp.dot(a, b, preferred_element_type=F32)


def dot_nt(a, b):
    return lax.dot_general(a, b, (((1,), (1,)), ((), ())), preferred_element_type=F32)


def resample_kernel(
    dest_ref, win_ref, choice_ref, weight_ref, raw_hbm, bank_ref, out_ref,
    raw_ref, rows_ref, held_ref, slot_win_ref, sems,
):
    tiles, blocks = held_ref.shape[0], dest_ref.shape[0]
    deep = BANDS * SRC_ROWS

    def fetch(group):
        part = pl.ds(group * STEP_BLOCKS, STEP_BLOCKS)
        return pltpu.make_async_copy(raw_hbm.at[part], raw_ref.at[part], sems.at[group])

    for group in range(blocks // STEP_BLOCKS):
        fetch(group).start()

    def clear(i, carry):
        held_ref[i] = 0
        for k in range(CAP):
            slot_win_ref[i * CAP + k] = -1
        return carry

    lax.fori_loop(0, tiles, clear, 0, unroll=8)

    turned = jnp.transpose(weight_ref[...].astype(F32)).astype(BF16)
    depth = lax.broadcasted_iota(jnp.int32, (WIN_ROWS * SRC_ROWS, 256), 0)
    lane = lax.broadcasted_iota(jnp.int32, (WIN_ROWS * SRC_ROWS, 256), 1)
    offset = depth - (lane & (SRC_ROWS - 1))
    for r in range(WIN_ROWS):
        wide = dot(turned, (offset == r * SRC_ROWS).astype(F32).astype(BF16))
        for h in range(2):
            rows_ref[h, pl.ds(r, blocks, stride=WIN_ROWS), :] = wide[:, h * 128:(h + 1) * 128]

    line = lax.broadcasted_iota(jnp.int32, (LINES, 256), 0)
    lane = lax.broadcasted_iota(jnp.int32, (LINES, 256), 1)
    own = (line >> 3) == (lane >> 4)
    spot = lax.broadcasted_iota(jnp.int32, (WIN_ROWS, TILE_COLS), 1)

    def work(group, carry):
        fetch(group).wait()
        rowed = []
        for j in range(STEP_BLOCKS):
            n = group * STEP_BLOCKS + j
            row = pl.multiple_of(n * WIN_ROWS, WIN_ROWS)
            rows = jnp.concatenate(
                [rows_ref[h, pl.ds(row, WIN_ROWS), :] for h in range(2)], axis=1
            )
            weights = jnp.where(own, jnp.concatenate([rows] * BANDS, axis=0), 0.0)
            rowed.append(dot(weights.astype(BF16)[:, 0:deep], raw_ref[n]).astype(BF16))
        done = []
        for j in range(STEP_BLOCKS):
            n = group * STEP_BLOCKS + j
            done.append(dot(rowed[j], bank_ref[choice_ref[n]]).astype(BF16))
        for j in range(STEP_BLOCKS):
            n = group * STEP_BLOCKS + j
            tile = dest_ref[n]
            rank = held_ref[tile]
            held_ref[tile] = rank + 1
            slot_win_ref[tile * CAP + rank] = win_ref[n]
            place = pl.ds(pl.multiple_of(rank * LINES, WIN_ROWS), LINES)
            out_ref[tile, place, :] = done[j]
        return carry

    lax.fori_loop(0, blocks // STEP_BLOCKS, work, 0)

    def number(i, carry):
        window = jnp.where(spot == 0, slot_win_ref[i * CAP], slot_win_ref[i * CAP + 1])
        out_ref[i, CAP * LINES:] = window.astype(F32).astype(BF16)
        return carry

    lax.fori_loop(0, tiles, number, 0, unroll=4)


def resample(granule_blocks, row_weights, column_bank, destination, window_index, bank_index, tiles):
    blocks = granule_blocks.shape[0]
    deep = BANDS * SRC_ROWS
    vmem = pl.BlockSpec(memory_space=pltpu.VMEM)
    smem = pl.BlockSpec(memory_space=pltpu.SMEM)
    return pl.pallas_call(
        resample_kernel,
        in_specs=[smem, smem, smem, vmem, pl.BlockSpec(memory_space=pl.ANY), vmem],
        out_specs=vmem,
        scratch_shapes=[
            pltpu.VMEM((blocks, deep, TILE_COLS), BF16),
            pltpu.VMEM((2, blocks * WIN_ROWS, 128), F32),
            pltpu.SMEM((tiles,), jnp.int32),
            pltpu.SMEM((tiles * CAP,), jnp.int32),
            pltpu.SemaphoreType.DMA((blocks // STEP_BLOCKS,)),
        ],
        out_shape=jax.ShapeDtypeStruct((tiles, PACKED, TILE_COLS), BF16),
        compiler_params=pltpu.CompilerParams(vmem_limit_bytes=60 * MIB),
        name="resample",
    )(
        destination, window_index, bank_index,
        row_weights.transpose(1, 2, 0).reshape(WIN_ROWS * SRC_ROWS, blocks),
        granule_blocks.reshape(blocks, deep, TILE_COLS),
        column_bank,
    )


def grid_kernel(
    got_hbm, perm_ref, grid_ref, lines_ref, left_ref, right_ref,
    got_ref, sum_ref, number_ref, win_ref, count_ref, sem, sems,
):
    tiles = got_ref.shape[0]
    size = tiles // PIECES
    last = pl.ds(CAP * LINES, WIN_ROWS)
    head = pltpu.make_async_copy(got_hbm.at[:, last], got_ref.at[:, last], sems.at[PIECES])
    head.start()

    def fetch(piece):
        part = pl.ds(piece * size, size), pl.ds(0, CAP * LINES)
        return pltpu.make_async_copy(got_hbm.at[part], got_ref.at[part], sems.at[piece])

    for piece in range(PIECES):
        fetch(piece).start()
    head.wait()
    numbers = got_ref[:, CAP * LINES:, :].astype(F32)
    number_ref[...] = jnp.max(numbers, axis=1).astype(jnp.int32)
    copy = pltpu.make_async_copy(number_ref, win_ref, sem)
    copy.start()

    def clear(w, carry):
        sum_ref[w] = jnp.zeros(sum_ref.shape[1:], F32)
        count_ref[w] = 0
        return carry

    lax.fori_loop(0, NWIN + 1, clear, 0)
    copy.wait()

    def add(t, carry):
        for k in range(CAP):
            w = win_ref[t, k]
            w = jnp.where(w < 0, NWIN, w)
            block = got_ref[t, k * LINES:(k + 1) * LINES].astype(F32)
            sum_ref[w, 0:LINES] = sum_ref[w, 0:LINES] + block
            count_ref[w] = count_ref[w] + 1
        return carry

    def add_piece(piece, carry):
        fetch(piece).wait()
        return lax.fori_loop(piece * size, (piece + 1) * size, add, carry)

    lax.fori_loop(0, PIECES, add_piece, 0)

    def finish(group, carry):
        first = group * GROUP
        means = []
        for k in range(GROUP):
            w = first + k
            divisor = jnp.maximum(count_ref[w], 1).astype(F32)
            mean = (sum_ref[w, 0:LINES] / divisor).astype(BF16).astype(F32)
            sum_ref[w, 0:LINES] = mean
            means.append(mean)
        row = pl.multiple_of(first * WIN_ROWS, GROUP * WIN_ROWS)
        for b in range(BANDS):
            part = jnp.concatenate([m[b * WIN_ROWS:(b + 1) * WIN_ROWS] for m in means], axis=0)
            grid_ref[b, pl.ds(row, GROUP * WIN_ROWS), :] = part.astype(BF16)
        for pair in range(GROUP // 2):
            lines = jnp.concatenate(
                [
                    sum_ref[first + pair * 2 + k, pl.ds(r, 16, stride=WIN_ROWS), :]
                    for k in range(2)
                    for r in range(WIN_ROWS)
                ],
                axis=0,
            ).astype(BF16)
            row = pl.multiple_of((first + pair * 2) * 128, 256)
            lines_ref[pl.ds(row, 256), :] = lines
            both = dot_nt(perm_ref[...], lines).astype(BF16)
            for k in range(2):
                w = first + pair * 2 + k
                turned = both[:, k * 128:(k + 1) * 128]
                left_ref[pl.ds(pl.multiple_of(w * 16, 16), 16), :] = turned[0:16]
                right_ref[pl.ds(pl.multiple_of(w * 16, 16), 16), :] = turned[16:32]
        return carry

    lax.fori_loop(0, NWIN // GROUP, finish, 0)


def grid(received):
    tiles = received.shape[0]
    perm = np.zeros((32, TILE_COLS), np.float32)
    for p in range(PHASES):
        for a in range(HALO):
            perm[p * HALO + a, a * PHASES + p] = 1.0
            perm[16 + p * HALO + a, (SPOTS - HALO + a) * PHASES + p] = 1.0
    vmem = pl.BlockSpec(memory_space=pltpu.VMEM)
    return pl.pallas_call(
        grid_kernel,
        in_specs=[pl.BlockSpec(memory_space=pl.ANY), vmem],
        out_specs=[vmem] * 4,
        out_shape=[
            jax.ShapeDtypeStruct((BANDS, NWIN * WIN_ROWS, TILE_COLS), BF16),
            jax.ShapeDtypeStruct((NWIN * 128, 128), BF16),
            jax.ShapeDtypeStruct((NWIN * 16, 128), BF16),
            jax.ShapeDtypeStruct((NWIN * 16, 128), BF16),
        ],
        scratch_shapes=[
            pltpu.VMEM(received.shape, BF16),
            pltpu.VMEM((NWIN + 1, 128, TILE_COLS), F32),
            pltpu.VMEM((tiles, TILE_COLS), jnp.int32),
            pltpu.SMEM((tiles, TILE_COLS), jnp.int32),
            pltpu.SMEM((NWIN + 1,), jnp.int32),
            pltpu.SemaphoreType.DMA,
            pltpu.SemaphoreType.DMA((PIECES + 1,)),
        ],
        compiler_params=pltpu.CompilerParams(vmem_limit_bytes=24 * MIB),
        name="grid",
    )(received, jnp.asarray(perm, BF16))


def turn_kernel(lines_ref, perm_ref, main_ref, lower_ref, top_ref, bottom_ref):
    def step(i, carry):
        for k in range(2):
            w = i * 2 + k
            start = pl.multiple_of(w * 128, 128)
            below = pl.multiple_of(jnp.minimum(w * 128 + 64, (NWIN - 1) * 128), 64)
            lines = jnp.concatenate(
                [lines_ref[pl.ds(start, 128), :], lines_ref[pl.ds(below, 128), :]], axis=0
            )
            both = dot_nt(perm_ref[...], lines).astype(BF16)
            main_ref[pl.ds(start, 128), :] = both[:, 0:128]
            lower_ref[pl.ds(start, 128), :] = both[:, 128:256]
        return carry

    lax.fori_loop(0, NWIN // 2, step, 0, unroll=2)
    top_ref[...] = main_ref[0:top_ref.shape[0]]
    bottom_ref[...] = main_ref[(NWIN - HALO) * 128:]


def turn(lines):
    perm = np.zeros((TILE_COLS, TILE_COLS), np.float32)
    for p in range(PHASES):
        for a in range(SPOTS):
            perm[p * SPOTS + a, a * PHASES + p] = 1.0
    vmem = pl.BlockSpec(memory_space=pltpu.VMEM)
    return pl.pallas_call(
        turn_kernel,
        in_specs=[vmem] * 2,
        out_specs=[vmem] * 4,
        out_shape=[
            jax.ShapeDtypeStruct((NWIN * 128, 128), BF16),
            jax.ShapeDtypeStruct((NWIN * 128, 128), BF16),
            jax.ShapeDtypeStruct(((HALO + 1) * 128, 128), BF16),
            jax.ShapeDtypeStruct((HALO * 128, 128), BF16),
        ],
        compiler_params=pltpu.CompilerParams(vmem_limit_bytes=16 * MIB),
        cost_estimate=pl.CostEstimate(
            flops=2 * NWIN * 128 ** 3 * 2, bytes_accessed=8 * MIB, transcendentals=0
        ),
        name="turn",
    )(lines, jnp.asarray(perm, BF16))


def exchange_columns(left, right):
    across = lax.axis_size("tx")
    right_ward = [(i, i + 1) for i in range(across - 1)]
    left_ward = [(t, s) for s, t in right_ward]
    return lax.ppermute(right, "tx", right_ward), lax.ppermute(left, "tx", left_ward)


def exchange_rows(top, bottom, from_left, from_right):
    down = lax.axis_size("ty")
    down_ward = [(i, i + 1) for i in range(down - 1)]
    up_ward = [(t, s) for s, t in down_ward]
    m, h = HALO * 128, HALO * 16
    first = jnp.concatenate([top[:m], from_left[:h], from_right[:h]], axis=0)
    last = jnp.concatenate([bottom, from_left[-h:], from_right[-h:]], axis=0)
    return lax.ppermute(last, "ty", down_ward), lax.ppermute(first, "ty", up_ward)


def spread_matrix():
    out = np.zeros((PHASES + 2, GROUP_POINTS, GROUP * 48), np.float32)
    for index in range(PHASES + 2):
        p = (index - 1) % PHASES
        shift = -1 if index == 0 else (1 if index == PHASES + 1 else 0)
        for k in range(GROUP):
            for a in range(WIDE):
                s = a + shift
                row = k * WIDE + a
                if s < 0 or s >= WIDE:
                    continue
                if s < HALO:
                    out[index, row, GROUP * 16 + k * 16 + p * HALO + s] = 1.0
                elif s < HALO + SPOTS:
                    out[index, row, k * 16 + s - HALO] = 1.0
                else:
                    out[index, row, GROUP * 32 + k * 16 + p * HALO + s - HALO - SPOTS] = 1.0
    return out


def relu(x):
    return jnp.maximum(x, 0.0)


def level_one(x1, x2, one_ref, down2_ref, store):
    for cb in range(4):
        for version, x in enumerate((x1, x2)):
            taps = jnp.concatenate([x[2 * cb + k] for k in range(4)], axis=1)
            level = relu(dot(taps, one_ref[...])).astype(BF16)
            for half in range(2):
                down = relu(dot(level[:, half * 256:(half + 1) * 256], down2_ref[...]))
                store(2 * version + half, cb, down)


def lay(spread, first, second):
    return dot(spread, jnp.concatenate([jnp.concatenate(p, axis=0) for p in (first, second)], axis=1))


def interior_kernel(
    main_ref, lower_ref, fl_ref, fr_ref, spread_ref, one_ref, down2_ref, out_ref, side_ref, x1, x2
):
    low = lax.broadcasted_iota(jnp.int32, (16, 128), 1) < 64
    for s, side in enumerate((fl_ref, fr_ref)):
        for w in range(NWIN - 1):
            after = side[(w + 1) * 16:(w + 2) * 16].astype(F32)
            both = jnp.where(low, after, side[w * 16:(w + 1) * 16].astype(F32))
            side_ref[s, w * 16:(w + 1) * 16] = pltpu.roll(both, 64, 1).astype(BF16)

    def place(g, carry):
        row = pl.multiple_of(g * GROUP_POINTS, GROUP_POINTS)
        w = g * GROUP + GROUP - HALO
        edge = [pl.ds(pl.multiple_of((w + k) * 16, 16), 16) for k in range(GROUP)]
        for index in range(PHASES + 2):
            p = (index - 1) % PHASES
            own = [
                pl.ds(pl.multiple_of((w + k) * 128 + p * 16, 16), 16) for k in range(GROUP)
            ]
            first = [main_ref[o, :] for o in own]
            first += [ref[e, :] for ref in (fl_ref, fr_ref) for e in edge]
            second = [lower_ref[o, :] for o in own]
            second += [side_ref[s, e, :] for s in range(2) for e in edge]
            laid = lay(spread_ref[index], first, second).astype(BF16)
            x1[index, pl.ds(row, GROUP_POINTS), :] = laid[:, 0:128]
            x2[index, pl.ds(row, GROUP_POINTS), :] = laid[:, 128:256]
        return carry

    lax.fori_loop(0, TALL // GROUP - 2, place, 0)

    def store(rb, cb, down):
        out_ref[rb, cb] = down.astype(BF16)

    level_one(x1, x2, one_ref, down2_ref, store)


def interior(main, lower, from_left, from_right, spread, one, down2):
    vmem = pl.BlockSpec(memory_space=pltpu.VMEM)
    points = POINTS - 2 * GROUP_POINTS
    return pl.pallas_call(
        interior_kernel,
        in_specs=[vmem] * 7,
        out_specs=vmem,
        out_shape=jax.ShapeDtypeStruct((4, 4, points, 128), BF16),
        scratch_shapes=[
            pltpu.VMEM((2, NWIN * 16, 128), BF16),
            pltpu.VMEM((PHASES + 2, points, 128), BF16),
            pltpu.VMEM((PHASES + 2, points, 128), BF16),
        ],
        compiler_params=pltpu.CompilerParams(vmem_limit_bytes=32 * MIB),
        cost_estimate=pl.CostEstimate(
            flops=2 * points * 8 * (512 * 512 + 512 * 256),
            bytes_accessed=16 * MIB,
            transcendentals=0,
        ),
        name="interior",
    )(main, lower, from_left, from_right, spread, one, down2)


def encoder_kernel(
    inner_hbm, top_ref, bottom_ref, fl_ref, fr_ref, above_ref, below_ref, spread_ref, one_ref,
    down2_ref, two_hbm, down3_hbm, three_hbm, down4_hbm, four_hbm,
    out_ref,
    inner_ref, ext1, ext2, x1, x2, d2, d3, d4, flat, stage,
    two_ref, down3_ref, three_ref, down4_ref, four_ref, sems,
):
    copies = [
        pltpu.make_async_copy(src, dst, sems.at[i])
        for i, (src, dst) in enumerate(
            (
                (down3_hbm, down3_ref),
                (three_hbm, three_ref),
                (down4_hbm, down4_ref),
                (four_hbm, four_ref),
                (inner_hbm, inner_ref),
                (two_hbm, two_ref),
            )
        )
    ]
    for i in (4, 5, 0, 1, 2, 3):
        copies[i].start()
    for side in range(2):
        for p in range(4):
            stage[side, p, 0:MARGIN] = jnp.zeros((MARGIN, 128), F32)
            stage[side, p, MARGIN + POINTS:] = jnp.zeros((MARGIN, 128), F32)

    m = HALO * 128
    for h in range(HALO):
        for source, i in ((above_ref, h), (below_ref, 3 * HALO + 1 + h)):
            ext1[i, 0:128] = source[h * 128:(h + 1) * 128]
            ext1[i, 128:144] = source[m + h * 16:m + h * 16 + 16]
            ext1[i, 144:160] = source[m + (HALO + h) * 16:m + (HALO + h) * 16 + 16]
    near = [(HALO + k, top_ref, k, k) for k in range(HALO + 1)]
    near += [(2 * HALO + 1 + k, bottom_ref, k, NWIN - HALO + k) for k in range(HALO)]
    for i, source, k, w in near:
        ext1[i, 0:128] = source[k * 128:(k + 1) * 128]
        ext1[i, 128:144] = fl_ref[w * 16:(w + 1) * 16]
        ext1[i, 144:160] = fr_ref[w * 16:(w + 1) * 16]

    low = lax.broadcasted_iota(jnp.int32, (160, 128), 1) < 64
    edges = (0, GROUP + 1)
    for base in edges:
        for k in range(GROUP):
            i = base + k
            after = min(i + 1, ext1.shape[0] - 1)
            both = jnp.where(low, ext1[after].astype(F32), ext1[i].astype(F32))
            ext2[i] = pltpu.roll(both, 64, 1).astype(BF16)

    for e, base in enumerate(edges):
        for index in range(PHASES + 2):
            p = (index - 1) % PHASES
            sides = []
            for ext in (ext1, ext2):
                pieces = [ext[base + k, p * 16:(p + 1) * 16] for k in range(GROUP)]
                pieces += [ext[base + k, 128:144] for k in range(GROUP)]
                pieces += [ext[base + k, 144:160] for k in range(GROUP)]
                sides.append(pieces)
            laid = lay(spread_ref[index], *sides).astype(BF16)
            x1[index, e * GROUP_POINTS:(e + 1) * GROUP_POINTS] = laid[:, 0:128]
            x2[index, e * GROUP_POINTS:(e + 1) * GROUP_POINTS] = laid[:, 128:256]

    across, below = lax.axis_size("tx"), lax.axis_size("ty")
    x, y = lax.axis_index("tx"), lax.axis_index("ty")
    least_w, most_w = jnp.where(y > 0, 0, HALO), jnp.where(y < below - 1, TALL, HALO + NWIN)
    least_a, most_a = jnp.where(x > 0, 0, HALO), jnp.where(x < across - 1, WIDE, HALO + SPOTS)
    point = lax.broadcasted_iota(jnp.int32, (POINTS, 128), 0)
    w = (point * (65536 // WIDE + 1)) >> 16
    a = point - w * WIDE
    inside = (w >= least_w) & (w < most_w) & (a >= least_a) & (a < most_a)
    mask = inside.astype(F32)
    mask2 = jnp.concatenate([mask, mask], axis=1)
    mask4 = jnp.concatenate([mask2, mask2], axis=1)

    def put(dst, i, j, value, last):
        rows = [(i + 1, 0)]
        if i == last:
            rows.append((0, WIDE))
        if i == 0:
            rows.append((last + 2, -WIDE))
        cols = [(j + 1, 0)]
        if j == last:
            cols.append((0, 1))
        if j == 0:
            cols.append((last + 2, -1))
        dst[i + 1, j + 1] = value.astype(BF16)
        side = (i + j) % 2
        for p in range(value.shape[1] // 128):
            lanes = slice(p * 128, (p + 1) * 128)
            stage[side, p, MARGIN:MARGIN + POINTS] = value[:, lanes]
            for r, row_shift in rows:
                for c, col_shift in cols:
                    shift = row_shift + col_shift
                    if shift:
                        moved = stage[side, p, MARGIN - shift:MARGIN - shift + POINTS]
                        dst[r, c, :, lanes] = moved.astype(BF16)

    copies[4].wait()

    def store(rb, cb, down):
        inner = inner_ref[rb, cb].astype(F32)
        down = jnp.concatenate([down[:GROUP_POINTS], inner, down[GROUP_POINTS:]], axis=0)
        if rb == 3:
            down = pltpu.roll(down, WIDE, 0)
        put(d2, (rb + 1) % 4, cb, down * mask, 3)

    level_one(x1, x2, one_ref, down2_ref, store)

    copies[5].wait()
    copies[0].wait()
    for rp in range(2):
        for j in range(2):
            total = None
            for v2 in range(2):
                taps = jnp.concatenate(
                    [d2[2 * rp + r, 2 * j + v2 + v] for r in range(4) for v in range(3)], axis=1
                )
                level = relu(dot(taps, two_ref[...])).astype(BF16)
                part = dot(level, down3_ref[v2])
                total = part if total is None else total + part
            put(d3, rp, j, relu(total) * mask2, 1)

    copies[1].wait()
    copies[2].wait()
    total = None
    for i in range(2):
        for j in range(2):
            taps = jnp.concatenate(
                [d3[i + u, j + v] for u in range(3) for v in range(3)], axis=1
            )
            level = relu(dot(taps, three_ref[...])).astype(BF16)
            part = dot(level, down4_ref[i * 2 + j])
            total = part if total is None else total + part
    put(d4, 0, 0, relu(total) * mask4, 0)

    copies[3].wait()
    first, count = HALO * WIDE, NWIN * WIDE
    taps = jnp.concatenate(
        [d4[u, v, first:first + count] for u in range(3) for v in range(3)], axis=1
    )
    flat[...] = relu(dot(taps, four_ref[...]))
    for w in range(NWIN):
        start = w * WIDE + HALO
        out_ref[w] = flat[start:start + SPOTS].astype(BF16)


def encoder(inner, edges, spread, one, down2, two, down3, three, down4, four):
    vmem = pl.BlockSpec(memory_space=pltpu.VMEM)
    hbm = pl.BlockSpec(memory_space=pl.ANY)
    rim = 2 * GROUP_POINTS
    return pl.pallas_call(
        encoder_kernel,
        in_specs=[hbm] + [vmem] * 9 + [hbm] * 5,
        out_specs=vmem,
        out_shape=jax.ShapeDtypeStruct((NWIN, SPOTS, four.shape[-1]), BF16),
        scratch_shapes=[
            pltpu.VMEM(inner.shape, BF16),
            pltpu.VMEM((2 * GROUP + 1, 160, 128), BF16),
            pltpu.VMEM((2 * GROUP + 1, 160, 128), BF16),
            pltpu.VMEM((PHASES + 2, rim, 128), BF16),
            pltpu.VMEM((PHASES + 2, rim, 128), BF16),
            pltpu.VMEM((6, 6, POINTS, 128), BF16),
            pltpu.VMEM((4, 4, POINTS, 256), BF16),
            pltpu.VMEM((3, 3, POINTS, 512), BF16),
            pltpu.VMEM((NWIN * WIDE, 512), F32),
            pltpu.VMEM((2, 4, POINTS + 2 * MARGIN, 128), F32),
            pltpu.VMEM(two.shape, BF16),
            pltpu.VMEM(down3.shape, BF16),
            pltpu.VMEM(three.shape, BF16),
            pltpu.VMEM(down4.shape, BF16),
            pltpu.VMEM(four.shape, BF16),
            pltpu.SemaphoreType.DMA((6,)),
        ],
        compiler_params=pltpu.CompilerParams(vmem_limit_bytes=44 * MIB),
        name="encoder",
    )(inner, *edges, spread, one, down2, two, down3, three, down4, four)


def level_one_weights(kernel):
    kernel = jnp.pad(kernel, ((0, 0), (0, 0), (0, 16 - BANDS), (0, 0)))
    columns = []
    for rb in range(2):
        for i in range(2):
            for j in range(2):
                top = 1 + 2 * rb + i
                wide = jnp.pad(kernel, ((top, 5 - top), (j, 1 - j), (0, 0), (0, 0)))
                columns.append(wide.transpose(1, 0, 2, 3).reshape(4 * 8 * 16, -1))
    return jnp.concatenate(columns, axis=1)


def level_two_weights(kernel):
    none = ((0, 0),) * 3
    pair = [jnp.pad(kernel, ((i, 1 - i),) + none) for i in range(2)]
    return jnp.concatenate(pair, axis=3).reshape(12 * kernel.shape[2], -1)


def body(
    granule_blocks, row_weights, column_bank, destination, window_index, bank_index,
    kernel_one, reduce_two, kernel_two, reduce_three, kernel_three, reduce_four, kernel_four,
):
    axes = ("tx", "ty")
    tiles = lax.axis_size("tx") * lax.axis_size("ty")
    slots = resample(
        granule_blocks, row_weights, column_bank, destination, window_index, bank_index, tiles
    )
    received = lax.all_to_all(slots, axes, split_axis=0, concat_axis=0, tiled=True)
    one = level_one_weights(kernel_one)
    two = level_two_weights(kernel_two)
    down3 = reduce_three.transpose(1, 0, 2, 3).reshape(2, 256, 256)
    received, one, two, down3 = lax.optimization_barrier((received, one, two, down3))
    gridded, lines, left, right = grid(received)
    from_left, from_right = exchange_columns(left, right)
    main, lower, top, bottom = turn(lines)
    above, below = exchange_rows(top, bottom, from_left, from_right)
    spread = jnp.asarray(spread_matrix(), BF16)
    down2 = reduce_two.reshape(256, 128)
    inner = interior(main, lower, from_left, from_right, spread, one, down2)
    flat = encoder(
        inner, (top, bottom, from_left, from_right, above, below), spread, one, down2,
        two, down3,
        kernel_three.reshape(9 * 256, 256),
        reduce_four.reshape(4, 256, 512),
        kernel_four.reshape(9 * 512, 512),
    )
    return gridded, flat.transpose(2, 0, 1)


def solution(mesh):
    both = P(("tx", "ty"))
    in_specs = (both, both, P(), both, both, both) + (P(),) * 7
    out_specs = (P(None, "ty", "tx"), P(None, "ty", "tx"))
    return jax.shard_map(body, mesh=mesh, in_specs=in_specs, out_specs=out_specs, check_vma=False)
```

profile of v0, /device:TPU:1, one launch (start us, length us, event | category | flops | bytes accessed | tf_op | source)
XLA Modules:
  0.0 100.1 jit_solution(15534889566632657097)
XLA Ops:
  0.6 6.1 %resample.1 = bf16[32,216,128]{2,1,0:T(8,128)(2,1)} custom-call(s32[64]{0:T(128)} %dest_ref.1, s32[64]{0:T(128)} %win_ref.1, s32[64]{0:T(128)} %choice_ref.1, bf16[128,64]{1,0:T(8,128)(2,1)} %bitcast.54, bf16[64,208,128]{2,1,0:T(8,128)(2,1)} %bitcast.43, bf16[8,128,128]{2,1,0:T(8,128)(2,1)} %bank_ref.1), custom_call_target="tpu_custom_call" | custom-call | tf_op jit(solution)/shard_map/resample/pallas_call | solution.py:119
  6.7 0.0 copy-start.7
  6.8 7.1 %all-to-all-start = ((bf16[32,216,128]{2,1,0:T(8,128)(2,1)}), bf16[32,216,128]{2,1,0:T(8,128)(2,1)S(1)}, u32[]{:S(2)}, u32[]{:S(2)}) async-start(bf16[32,216,128]{2,1,0:T(8,128)(2,1)} %resample.1), calls=%async_computation | async-start | bytes 3538944 | tf_op jit(solution)/shard_map/all_to_all | solution.py:615
  13.9 0.0 copy-start.6
  13.9 0.2 pad_bitcast_fusion
  14.2 0.7 copy.24
  14.9 0.7 copy.25
  15.6 1.3 %concatenate.12.one_ref = bf16[512,512]{1,0:T(8,128)(2,1)S(1)} concatenate(bf16[512,64]{1,0:T(8,128)(2,1)S(1)} %bitcast.45, bf16[512,64]{1,0:T(8,128)(2,1)S(1)} %bitcast.46, bf16[512,64]{1,0:T(8,128)(2,1)S(1)} %bitcast.47, bf16[512,64]{1,0:T(8,128)(2,1)S(1)} %bitcast.48, bf16[512,64]{1,0:T(8,128)(2,1)S(1)} %bitcast.49, bf16[512,64]{1,0:T(8,128)(2,1)S(1)} %bitcast.50, ...), dimensions={1} | concatenate | bytes 1048576 | tf_op jit(solution)/shard_map/concatenate | solution.py:597
  16.9 0.0 copy-start.4
  16.9 1.1 %fusion.2 = bf16[4,3,128,256]{3,2,1,0:T(8,128)(2,1)S(1)} fusion(bf16[3,3,128,128]{3,2,1,0:T(8,128)(2,1)} %param.24), kind=kLoop, calls=%fused_computation.4 | loop fusion | flops 3145728 | bytes 1081344 | tf_op jit(solution)/shard_map/concatenate | solution.py:603
  18.1 38.3 %all-to-all-done.got_hbm = bf16[32,216,128]{2,1,0:T(8,128)(2,1)S(1)} async-done(((bf16[32,216,128]{2,1,0:T(8,128)(2,1)}), bf16[32,216,128]{2,1,0:T(8,128)(2,1)S(1)}, u32[]{:S(2)}, u32[]{:S(2)}) %all-to-all-start) | async-done | bytes 1769504 | tf_op jit(solution)/shard_map/all_to_all | solution.py:615
  56.3 4.3 %grid.1 = (bf16[13,256,128]{2,1,0:T(8,128)(2,1)}, bf16[4096,128]{1,0:T(8,128)(2,1)S(1)}, bf16[512,128]{1,0:T(8,128)(2,1)S(1)}, bf16[512,128]{1,0:T(8,128)(2,1)S(1)}) custom-call(bf16[32,216,128]{2,1,0:T(8,128)(2,1)S(1)} %all-to-all-done.got_hbm, bf16[32,128]{1,0:T(8,128)(2,1)S(1)} %copy-done.5), custom_call_target="tpu_custom_call" | custom-call | tf_op jit(solution)/shard_map/grid/pallas_call | solution.py:229
  60.6 2.8 %collective-permute-start.1 = (bf16[512,128]{1,0:T(8,128)(2,1)S(1)}, bf16[512,128]{1,0:T(8,128)(2,1)S(1)}, u32[]{:S(2)}, u32[]{:S(2)}) collective-permute-start(bf16[512,128]{1,0:T(8,128)(2,1)S(1)} %get-tuple-element.20), channel_id=1, source_target_pairs={{8,0},{16,8},{24,16},{9,1},{17,9},{25,17},{10,2},{18,10},{26,18},{... | collective-permute-start | bytes 393224 | tf_op jit(solution)/shard_map/ppermute | solution.py:300
  63.4 2.8 %collective-permute-start = (bf16[512,128]{1,0:T(8,128)(2,1)S(1)}, bf16[512,128]{1,0:T(8,128)(2,1)S(1)}, u32[]{:S(2)}, u32[]{:S(2)}) collective-permute-start(bf16[512,128]{1,0:T(8,128)(2,1)S(1)} %get-tuple-element.19), channel_id=1, source_target_pairs={{0,8},{8,16},{16,24},{1,9},{9,17},{17,25},{2,10},{10,18},{18,26},{... | collective-permute-start | bytes 393224 | tf_op jit(solution)/shard_map/ppermute | solution.py:300
  66.2 1.9 %turn.1 = (bf16[4096,128]{1,0:T(8,128)(2,1)S(1)}, bf16[4096,128]{1,0:T(8,128)(2,1)S(1)}, bf16[384,128]{1,0:T(8,128)(2,1)S(1)}, bf16[256,128]{1,0:T(8,128)(2,1)S(1)}) custom-call(bf16[4096,128]{1,0:T(8,128)(2,1)S(1)} %get-tuple-element.16.lines_ref, bf16[128,128]{1,0:T(8,128)(2,1)S(1)} %copy-done.4), custom_call_target="tpu_custom_call" | custom-call | flops 268435456 | bytes 8388608 | tf_op jit(solution)/shard_map/turn/pallas_call | solution.py:278
  68.2 0.0 collective-permute-done.1.fr_ref
  68.2 0.0 collective-permute-done.fl_ref
  68.2 2.8 %collective-permute-start.2 = (bf16[320,128]{1,0:T(8,128)(2,1)S(1)}, bf16[320,128]{1,0:T(8,128)(2,1)S(1)}, u32[]{:S(2)}, u32[]{:S(2)}) collective-permute-start(bf16[320,128]{1,0:T(8,128)(2,1)S(1)} %pad_maximum_fusion), channel_id=1, source_target_pairs={{0,1},{1,2},{2,3},{3,4},{4,5},{5,6},{6,7},{8,9},{9,10},{10,11},{11... | collective-permute-start | bytes 245768 | tf_op jit(solution)/shard_map/ppermute | solution.py:310
  71.0 1.3 %collective-permute-start.3 = (bf16[320,128]{1,0:T(8,128)(2,1)S(1)}, bf16[320,128]{1,0:T(8,128)(2,1)S(1)}, u32[]{:S(2)}, u32[]{:S(2)}) collective-permute-start(bf16[320,128]{1,0:T(8,128)(2,1)S(1)} %pad_maximum_fusion.1), channel_id=1, source_target_pairs={{1,0},{2,1},{3,2},{4,3},{5,4},{6,5},{7,6},{9,8},{10,9},{11,10},{12... | collective-permute-start | bytes 245768 | tf_op jit(solution)/shard_map/ppermute | solution.py:310
  72.3 0.0 copy-start
  72.4 0.0 copy-start.1
  72.4 5.9 %interior.1.inner_hbm = bf16[4,4,560,128]{3,2,1,0:T(8,128)(2,1)S(1)} custom-call(bf16[4096,128]{1,0:T(8,128)(2,1)S(1)} %get-tuple-element.17.main_ref, bf16[4096,128]{1,0:T(8,128)(2,1)S(1)} %get-tuple-element.18.lower_ref, bf16[512,128]{1,0:T(8,128)(2,1)S(1)} %collective-permute-done.fl_ref, bf16[512,128]{1,0:T(8,128)(2,1)S(1)} %collective-permute-done.1.fr_ref, ...), custom_call_target="tpu_custom_call" | custom-call | flops 3523215360 | bytes 16777216 | tf_op jit(solution)/shard_map/interior/pallas_call | solution.py:390
  78.3 0.0 collective-permute-done.3.below_ref
  78.3 21.7 %encoder.1 = bf16[32,16,512]{2,1,0:T(8,128)(2,1)} custom-call(bf16[4,4,560,128]{3,2,1,0:T(8,128)(2,1)S(1)} %interior.1.inner_hbm, bf16[384,128]{1,0:T(8,128)(2,1)S(1)} %get-tuple-element.22.top_ref, bf16[256,128]{1,0:T(8,128)(2,1)S(1)} %get-tuple-element.23.bottom_ref, bf16[512,128]{1,0:T(8,128)(2,1)S(1)} %collective-permute-done.fl_ref, ...), custom_call_target="tpu_custom_call" | custom-call | tf_op jit(solution)/shard_map/encoder/pallas_call | solution.py:560
  (25 shorter events, 0.1 us)
Async XLA Ops:
  6.7 7.1 %copy-start.7 = (bf16[3,3,13,64]{3,2,1,0:T(8,128)(2,1)S(1)}, bf16[3,3,13,64]{3,2,1,0:T(8,128)(2,1)}, u32[]{:S(2)}) copy-start(bf16[3,3,13,64]{3,2,1,0:T(8,128)(2,1)} %param.22) | copy-start | bytes 44932
  6.8 49.6 %all-to-all-start = ((bf16[32,216,128]{2,1,0:T(8,128)(2,1)}), bf16[32,216,128]{2,1,0:T(8,128)(2,1)S(1)}, u32[]{:S(2)}, u32[]{:S(2)}) async-start(bf16[32,216,128]{2,1,0:T(8,128)(2,1)} %resample.1), calls=%async_computation | async-start | bytes 3538944 | tf_op jit(solution)/shard_map/all_to_all | solution.py:615
  13.9 1.7 %copy-start.6 = (bf16[2,2,128,256]{3,2,1,0:T(8,128)(2,1)S(1)}, bf16[2,2,128,256]{3,2,1,0:T(8,128)(2,1)}, u32[]{:S(2)}) copy-start(bf16[2,2,128,256]{3,2,1,0:T(8,128)(2,1)} %param.25) | copy-start | bytes 786436
  15.6 40.7 %copy-start.5 = (bf16[32,128]{1,0:T(8,128)(2,1)S(1)}, bf16[32,128]{1,0:T(8,128)(2,1)}, u32[]{:S(2)}) copy-start(bf16[32,128]{1,0:T(8,128)(2,1)} %constant.9.clone.perm_ref) | copy-start | bytes 24580
  16.9 49.3 %copy-start.4 = (bf16[128,128]{1,0:T(8,128)(2,1)S(1)}, bf16[128,128]{1,0:T(8,128)(2,1)}, u32[]{:S(2)}) copy-start(bf16[128,128]{1,0:T(8,128)(2,1)} %constant.10.clone.perm_ref) | copy-start | bytes 98308
  56.3 16.0 %copy-start.2 = (bf16[10,80,192]{2,1,0:T(8,128)(2,1)S(1)}, bf16[10,80,192]{2,1,0:T(8,128)(2,1)}, u32[]{:S(2)}) copy-start(bf16[10,80,192]{2,1,0:T(8,128)(2,1)} %constant.11.clone.spread_ref) | copy-start | bytes 921604
  56.3 16.0 %copy-start.3 = (bf16[2,2,64,128]{3,2,1,0:T(8,128)(2,1)S(1)}, bf16[2,2,64,128]{3,2,1,0:T(8,128)(2,1)}, u32[]{:S(2)}) copy-start(bf16[2,2,64,128]{3,2,1,0:T(8,128)(2,1)} %param.23) | copy-start | bytes 196612
  60.6 7.5 %collective-permute-start.1 = (bf16[512,128]{1,0:T(8,128)(2,1)S(1)}, bf16[512,128]{1,0:T(8,128)(2,1)S(1)}, u32[]{:S(2)}, u32[]{:S(2)}) collective-permute-start(bf16[512,128]{1,0:T(8,128)(2,1)S(1)} %get-tuple-element.20), channel_id=1, source_target_pairs={{8,0},{16,8},{24,16},{9,1},{17,9},{25,17},{10,2},{18,10},{26,18},{... | collective-permute-start | bytes 393224 | tf_op jit(solution)/shard_map/ppermute | solution.py:300
  63.4 4.8 %collective-permute-start = (bf16[512,128]{1,0:T(8,128)(2,1)S(1)}, bf16[512,128]{1,0:T(8,128)(2,1)S(1)}, u32[]{:S(2)}, u32[]{:S(2)}) collective-permute-start(bf16[512,128]{1,0:T(8,128)(2,1)S(1)} %get-tuple-element.19), channel_id=1, source_target_pairs={{0,8},{8,16},{16,24},{1,9},{9,17},{17,25},{2,10},{10,18},{18,26},{... | collective-permute-start | bytes 393224 | tf_op jit(solution)/shard_map/ppermute | solution.py:300
  68.2 10.1 %collective-permute-start.2 = (bf16[320,128]{1,0:T(8,128)(2,1)S(1)}, bf16[320,128]{1,0:T(8,128)(2,1)S(1)}, u32[]{:S(2)}, u32[]{:S(2)}) collective-permute-start(bf16[320,128]{1,0:T(8,128)(2,1)S(1)} %pad_maximum_fusion), channel_id=1, source_target_pairs={{0,1},{1,2},{2,3},{3,4},{4,5},{5,6},{6,7},{8,9},{9,10},{10,11},{11... | collective-permute-start | bytes 245768 | tf_op jit(solution)/shard_map/ppermute | solution.py:310
  71.0 7.3 %collective-permute-start.3 = (bf16[320,128]{1,0:T(8,128)(2,1)S(1)}, bf16[320,128]{1,0:T(8,128)(2,1)S(1)}, u32[]{:S(2)}, u32[]{:S(2)}) collective-permute-start(bf16[320,128]{1,0:T(8,128)(2,1)S(1)} %pad_maximum_fusion.1), channel_id=1, source_target_pairs={{1,0},{2,1},{3,2},{4,3},{5,4},{6,5},{7,6},{9,8},{10,9},{11,10},{12... | collective-permute-start | bytes 245768 | tf_op jit(solution)/shard_map/ppermute | solution.py:310
  72.3 6.0 %copy-start = (bf16[3,3,256,256]{3,2,1,0:T(8,128)(2,1)S(1)}, bf16[3,3,256,256]{3,2,1,0:T(8,128)(2,1)}, u32[]{:S(2)}) copy-start(bf16[3,3,256,256]{3,2,1,0:T(8,128)(2,1)} %param.26) | copy-start | bytes 3538948
  72.4 6.0 %copy-start.1 = (bf16[2,2,256,512]{3,2,1,0:T(8,128)(2,1)S(1)}, bf16[2,2,256,512]{3,2,1,0:T(8,128)(2,1)}, u32[]{:S(2)}) copy-start(bf16[2,2,256,512]{3,2,1,0:T(8,128)(2,1)} %param.27) | copy-start | bytes 3145732
where the time goes:
time: 102 us; the launch traced here: 100 us
  Pallas kernels  39.9 us (39%)
  waiting for transfers between devices  38.3 us (38%)
  starting transfers between devices  16.7 us (16%)
  local copies, waits for them, and re-layouts  3.01 us (3%)
  other arithmetic  1.14 us (1%)
  between operations  1.11 us (1%)
    all_to_all x1, waiting for transfers between devices, body(): lax.all_to_all(slots, axes, split_axis=0, concat_axis=0, tiled=True)  38.3 us
    pallas_call x1, Pallas kernels, encoder(): pl.pallas_call(encoder_kernel, in_specs=[hbm] + [vmem] * 9 + [hbm] * 5, o...  21.7 us
    all_to_all x1, starting transfers between devices, body(): lax.all_to_all(slots, axes, split_axis=0, concat_axis=0, tiled=True)  7.1 us
    pallas_call x1, Pallas kernels, resample(): pl.pallas_call(resample_kernel, in_specs=[smem, smem, smem, vmem, pl.Bloc...  6.1 us
    pallas_call x1, Pallas kernels, interior(): pl.pallas_call(interior_kernel, in_specs=[vmem] * 7, out_specs=vmem, out_...  5.92 us
    pallas_call x1, Pallas kernels, grid(): pl.pallas_call(grid_kernel, in_specs=[pl.BlockSpec(memory_space=pl.ANY),...  4.29 us
    ppermute x1, starting transfers between devices, exchange_columns(): lax.ppermute(right, 'tx', right_ward)  2.8 us
    ppermute x1, starting transfers between devices, exchange_rows(): lax.ppermute(last, 'ty', down_ward)  2.78 us
  transfers between devices with their start and end apart: 5, of which 1 were waited for; matrix products, arithmetic and copies ran while one was open for 4% of the time, Pallas kernels for 8%

commit v1 on v0

--- a/solution.py
+++ b/solution.py
@@ -519,27 +519,20 @@
     copies[0].wait()
     for rp in range(2):
         for j in range(2):
-            total = None
-            for v2 in range(2):
-                taps = jnp.concatenate(
-                    [d2[2 * rp + r, 2 * j + v2 + v] for r in range(4) for v in range(3)], axis=1
-                )
-                level = relu(dot(taps, two_ref[...])).astype(BF16)
-                part = dot(level, down3_ref[v2])
-                total = part if total is None else total + part
-            put(d3, rp, j, relu(total) * mask2, 1)
+            taps = jnp.concatenate(
+                [d2[2 * rp + r, 2 * j + c] for r in range(4) for c in range(4)], axis=1
+            )
+            level = relu(dot(taps, two_ref[...])).astype(BF16)
+            put(d3, rp, j, relu(dot(level, down3_ref[...])) * mask2, 1)
 
     copies[1].wait()
     copies[2].wait()
     total = None
     for i in range(2):
-        for j in range(2):
-            taps = jnp.concatenate(
-                [d3[i + u, j + v] for u in range(3) for v in range(3)], axis=1
-            )
-            level = relu(dot(taps, three_ref[...])).astype(BF16)
-            part = dot(level, down4_ref[i * 2 + j])
-            total = part if total is None else total + part
+        taps = jnp.concatenate([d3[i + u, c] for u in range(3) for c in range(4)], axis=1)
+        level = relu(dot(taps, three_ref[...])).astype(BF16)
+        part = dot(level, down4_ref[i])
+        total = part if total is None else total + part
     put(d4, 0, 0, relu(total) * mask4, 0)
 
     copies[3].wait()
@@ -597,10 +590,14 @@
     return jnp.concatenate(columns, axis=1)
 
 
-def level_two_weights(kernel):
-    none = ((0, 0),) * 3
-    pair = [jnp.pad(kernel, ((i, 1 - i),) + none) for i in range(2)]
-    return jnp.concatenate(pair, axis=3).reshape(12 * kernel.shape[2], -1)
+def block_weights(kernel, rows, cols):
+    none = ((0, 0), (0, 0))
+    parts = [
+        jnp.pad(kernel, ((i, rows - 1 - i), (j, cols - 1 - j)) + none)
+        for j in range(cols)
+        for i in range(rows)
+    ]
+    return jnp.concatenate(parts, axis=3).reshape(-1, rows * cols * kernel.shape[3])
 
 
 def body(
@@ -614,9 +611,10 @@
     )
     received = lax.all_to_all(slots, axes, split_axis=0, concat_axis=0, tiled=True)
     one = level_one_weights(kernel_one)
-    two = level_two_weights(kernel_two)
-    down3 = reduce_three.transpose(1, 0, 2, 3).reshape(2, 256, 256)
-    received, one, two, down3 = lax.optimization_barrier((received, one, two, down3))
+    two = block_weights(kernel_two, 2, 2)
+    three = block_weights(kernel_three, 1, 2)
+    down3 = reduce_three.transpose(1, 0, 2, 3).reshape(512, 256)
+    received, one, two, three, down3 = lax.optimization_barrier((received, one, two, three, down3))
     gridded, lines, left, right = grid(received)
     from_left, from_right = exchange_columns(left, right)
     main, lower, top, bottom = turn(lines)
@@ -626,9 +624,8 @@
     inner = interior(main, lower, from_left, from_right, spread, one, down2)
     flat = encoder(
         inner, (top, bottom, from_left, from_right, above, below), spread, one, down2,
-        two, down3,
-        kernel_three.reshape(9 * 256, 256),
-        reduce_four.reshape(4, 256, 512),
+        two, down3, three,
+        reduce_four.reshape(2, 512, 512),
         kernel_four.reshape(9 * 512, 512),
     )
     return gridded, flat.transpose(2, 0, 1)

time: 102 us -> 103 us (level)
  other arithmetic: 1.14 us -> 3.3 us
  local copies, waits for them, and re-layouts: 3.01 us -> 1.21 us
    concatenate x1 -> x2, other arithmetic: 1.12 us -> 3.28 us  [block_weights(): jnp.concatenate(parts, axis=3).reshape(-1, rows * cols * kernel.shape[3])]
    transpose x9, local copies, waits for them, and re-layouts: 1.62 us -> 0.31 us  [level_one_weights(): columns.append(wide.transpose(1, 0, 2, 3).reshape(4 * 8 * 16, -1))]
where the time goes in v1:
time: 103 us; the launch traced here: 101 us
  Pallas kernels  40.9 us (40%)
  waiting for transfers between devices  37.9 us (37%)
  starting transfers between devices  16.8 us (16%)
  other arithmetic  3.3 us (3%)
  local copies, waits for them, and re-layouts  1.21 us (1%)
  between operations  1.12 us (1%)
    all_to_all x1, waiting for transfers between devices, body(): lax.all_to_all(slots, axes, split_axis=0, concat_axis=0, tiled=True)  37.9 us
    pallas_call x1, Pallas kernels, encoder(): pl.pallas_call(encoder_kernel, in_specs=[hbm] + [vmem] * 9 + [hbm] * 5, o...  22.1 us
    all_to_all x1, starting transfers between devices, body(): lax.all_to_all(slots, axes, split_axis=0, concat_axis=0, tiled=True)  7.15 us
    pallas_call x1, Pallas kernels, resample(): pl.pallas_call(resample_kernel, in_specs=[smem, smem, smem, vmem, pl.Bloc...  6.12 us
    pallas_call x1, Pallas kernels, interior(): pl.pallas_call(interior_kernel, in_specs=[vmem] * 7, out_specs=vmem, out_...  5.92 us
    pallas_call x1, Pallas kernels, grid(): pl.pallas_call(grid_kernel, in_specs=[pl.BlockSpec(memory_space=pl.ANY),...  4.82 us
    concatenate x2, other arithmetic, block_weights(): jnp.concatenate(parts, axis=3).reshape(-1, rows * cols * kernel.shape[3])  3.28 us
    ppermute x1, starting transfers between devices, exchange_columns(): lax.ppermute(right, 'tx', right_ward)  2.8 us
  transfers between devices with their start and end apart: 5, of which 1 were waited for; matrix products, arithmetic and copies ran while one was open for 4% of the time, Pallas kernels for 8%

profile of v1, /device:TPU:1, one launch (start us, length us, event | category | flops | bytes accessed | tf_op | source)
XLA Modules:
  0.0 101.3 jit_solution(4000988484589320775)
XLA Ops:
  0.6 0.0 copy-start.7
  0.6 6.1 %resample.1 = bf16[32,216,128]{2,1,0:T(8,128)(2,1)} custom-call(s32[64]{0:T(128)} %dest_ref.1, s32[64]{0:T(128)} %win_ref.1, s32[64]{0:T(128)} %choice_ref.1, bf16[128,64]{1,0:T(8,128)(2,1)} %bitcast.54, bf16[64,208,128]{2,1,0:T(8,128)(2,1)} %bitcast.43, bf16[8,128,128]{2,1,0:T(8,128)(2,1)} %bank_ref.1), custom_call_target="tpu_custom_call" | custom-call | tf_op jit(solution)/shard_map/resample/pallas_call | solution.py:119
  6.8 0.0 copy-start.6
  6.8 7.2 %all-to-all-start = ((bf16[32,216,128]{2,1,0:T(8,128)(2,1)}), bf16[32,216,128]{2,1,0:T(8,128)(2,1)}, u32[]{:S(2)}, u32[]{:S(2)}) async-start(bf16[32,216,128]{2,1,0:T(8,128)(2,1)} %resample.1), calls=%async_computation | async-start | bytes 3538944 | tf_op jit(solution)/shard_map/all_to_all | solution.py:612
  13.9 0.0 copy-start.5
  14.0 0.2 pad_bitcast_fusion
  14.4 0.5 concatenate.15.one_ref
  14.9 0.3 copy-done.5
  15.2 1.8 %fusion.8 = bf16[3,4,256,512]{3,2,1,0:T(8,128)(2,1)} fusion(bf16[3,3,256,256]{3,2,1,0:T(8,128)(2,1)S(1)} %copy-done.5), kind=kLoop, calls=%fused_computation.16 | loop fusion | flops 12582912 | bytes 4325376 | tf_op jit(solution)/shard_map/concatenate | solution.py:600
  17.0 1.5 %fusion.10 = bf16[4,4,128,512]{3,2,1,0:T(8,128)(2,1)S(1)} fusion(bf16[3,3,128,128]{3,2,1,0:T(8,128)(2,1)} %param.24), kind=kLoop, calls=%fused_computation.18 | loop fusion | flops 20971520 | bytes 2392064 | tf_op jit(solution)/shard_map/concatenate | solution.py:600
  18.5 37.9 %all-to-all-done.got_hbm = bf16[32,216,128]{2,1,0:T(8,128)(2,1)} async-done(((bf16[32,216,128]{2,1,0:T(8,128)(2,1)}), bf16[32,216,128]{2,1,0:T(8,128)(2,1)}, u32[]{:S(2)}, u32[]{:S(2)}) %all-to-all-start) | async-done | bytes 1769504 | tf_op jit(solution)/shard_map/all_to_all | solution.py:612
  56.5 4.8 %grid.1 = (bf16[13,256,128]{2,1,0:T(8,128)(2,1)}, bf16[4096,128]{1,0:T(8,128)(2,1)S(1)}, bf16[512,128]{1,0:T(8,128)(2,1)S(1)}, bf16[512,128]{1,0:T(8,128)(2,1)S(1)}) custom-call(bf16[32,216,128]{2,1,0:T(8,128)(2,1)} %all-to-all-done.got_hbm, bf16[32,128]{1,0:T(8,128)(2,1)S(1)} %copy-done.4), custom_call_target="tpu_custom_call" | custom-call | tf_op jit(solution)/shard_map/grid/pallas_call | solution.py:229
  61.3 2.8 %collective-permute-start.1 = (bf16[512,128]{1,0:T(8,128)(2,1)S(1)}, bf16[512,128]{1,0:T(8,128)(2,1)S(1)}, u32[]{:S(2)}, u32[]{:S(2)}) collective-permute-start(bf16[512,128]{1,0:T(8,128)(2,1)S(1)} %get-tuple-element.21), channel_id=1, source_target_pairs={{8,0},{16,8},{24,16},{9,1},{17,9},{25,17},{10,2},{18,10},{26,18},{... | collective-permute-start | bytes 393224 | tf_op jit(solution)/shard_map/ppermute | solution.py:300
  64.1 2.8 %collective-permute-start = (bf16[512,128]{1,0:T(8,128)(2,1)S(1)}, bf16[512,128]{1,0:T(8,128)(2,1)S(1)}, u32[]{:S(2)}, u32[]{:S(2)}) collective-permute-start(bf16[512,128]{1,0:T(8,128)(2,1)S(1)} %get-tuple-element.20), channel_id=1, source_target_pairs={{0,8},{8,16},{16,24},{1,9},{9,17},{17,25},{2,10},{10,18},{18,26},{... | collective-permute-start | bytes 393224 | tf_op jit(solution)/shard_map/ppermute | solution.py:300
  66.9 1.9 %turn.1 = (bf16[4096,128]{1,0:T(8,128)(2,1)S(1)}, bf16[4096,128]{1,0:T(8,128)(2,1)S(1)}, bf16[384,128]{1,0:T(8,128)(2,1)S(1)}, bf16[256,128]{1,0:T(8,128)(2,1)S(1)}) custom-call(bf16[4096,128]{1,0:T(8,128)(2,1)S(1)} %get-tuple-element.17.lines_ref, bf16[128,128]{1,0:T(8,128)(2,1)S(1)} %copy-done.3), custom_call_target="tpu_custom_call" | custom-call | flops 268435456 | bytes 8388608 | tf_op jit(solution)/shard_map/turn/pallas_call | solution.py:278
  68.8 0.0 collective-permute-done.1.fr_ref
  68.8 0.0 collective-permute-done.fl_ref
  68.9 2.8 %collective-permute-start.2 = (bf16[320,128]{1,0:T(8,128)(2,1)S(1)}, bf16[320,128]{1,0:T(8,128)(2,1)S(1)}, u32[]{:S(2)}, u32[]{:S(2)}) collective-permute-start(bf16[320,128]{1,0:T(8,128)(2,1)S(1)} %pad_maximum_fusion), channel_id=1, source_target_pairs={{0,1},{1,2},{2,3},{3,4},{4,5},{5,6},{6,7},{8,9},{9,10},{10,11},{11... | collective-permute-start | bytes 245768 | tf_op jit(solution)/shard_map/ppermute | solution.py:310
  71.7 1.3 %collective-permute-start.3 = (bf16[320,128]{1,0:T(8,128)(2,1)S(1)}, bf16[320,128]{1,0:T(8,128)(2,1)S(1)}, u32[]{:S(2)}, u32[]{:S(2)}) collective-permute-start(bf16[320,128]{1,0:T(8,128)(2,1)S(1)} %pad_maximum_fusion.1), channel_id=1, source_target_pairs={{1,0},{2,1},{3,2},{4,3},{5,4},{6,5},{7,6},{9,8},{10,9},{11,10},{12... | collective-permute-start | bytes 245768 | tf_op jit(solution)/shard_map/ppermute | solution.py:310
  73.0 0.0 copy-start
  73.0 5.9 %interior.1.inner_hbm = bf16[4,4,560,128]{3,2,1,0:T(8,128)(2,1)S(1)} custom-call(bf16[4096,128]{1,0:T(8,128)(2,1)S(1)} %get-tuple-element.18.main_ref, bf16[4096,128]{1,0:T(8,128)(2,1)S(1)} %get-tuple-element.19.lower_ref, bf16[512,128]{1,0:T(8,128)(2,1)S(1)} %collective-permute-done.fl_ref, bf16[512,128]{1,0:T(8,128)(2,1)S(1)} %collective-permute-done.1.fr_ref, ...), custom_call_target="tpu_custom_call" | custom-call | flops 3523215360 | bytes 16777216 | tf_op jit(solution)/shard_map/interior/pallas_call | solution.py:390
  79.0 0.0 collective-permute-done.2.above_ref
  79.0 0.0 collective-permute-done.3.below_ref
  79.0 22.1 %encoder.1 = bf16[32,16,512]{2,1,0:T(8,128)(2,1)} custom-call(bf16[4,4,560,128]{3,2,1,0:T(8,128)(2,1)S(1)} %interior.1.inner_hbm, bf16[384,128]{1,0:T(8,128)(2,1)S(1)} %get-tuple-element.23.top_ref, bf16[256,128]{1,0:T(8,128)(2,1)S(1)} %get-tuple-element.24.bottom_ref, bf16[512,128]{1,0:T(8,128)(2,1)S(1)} %collective-permute-done.fl_ref, ...), custom_call_target="tpu_custom_call" | custom-call | tf_op jit(solution)/shard_map/encoder/pallas_call | solution.py:553
  (26 shorter events, 0.2 us)
Async XLA Ops:
  0.6 13.3 %copy-start.7 = (bf16[3,3,13,64]{3,2,1,0:T(8,128)(2,1)S(1)}, bf16[3,3,13,64]{3,2,1,0:T(8,128)(2,1)}, u32[]{:S(2)}) copy-start(bf16[3,3,13,64]{3,2,1,0:T(8,128)(2,1)} %param.22) | copy-start | bytes 44932
  6.8 7.6 %copy-start.6 = (bf16[2,2,128,256]{3,2,1,0:T(8,128)(2,1)S(1)}, bf16[2,2,128,256]{3,2,1,0:T(8,128)(2,1)}, u32[]{:S(2)}) copy-start(bf16[2,2,128,256]{3,2,1,0:T(8,128)(2,1)} %param.25) | copy-start | bytes 786436
  6.8 49.7 %all-to-all-start = ((bf16[32,216,128]{2,1,0:T(8,128)(2,1)}), bf16[32,216,128]{2,1,0:T(8,128)(2,1)}, u32[]{:S(2)}, u32[]{:S(2)}) async-start(bf16[32,216,128]{2,1,0:T(8,128)(2,1)} %resample.1), calls=%async_computation | async-start | bytes 3538944 | tf_op jit(solution)/shard_map/all_to_all | solution.py:612
  13.9 1.3 %copy-start.5 = (bf16[3,3,256,256]{3,2,1,0:T(8,128)(2,1)S(1)}, bf16[3,3,256,256]{3,2,1,0:T(8,128)(2,1)}, u32[]{:S(2)}) copy-start(bf16[3,3,256,256]{3,2,1,0:T(8,128)(2,1)} %param.26) | copy-start | bytes 3538948
  15.2 41.2 %copy-start.4 = (bf16[32,128]{1,0:T(8,128)(2,1)S(1)}, bf16[32,128]{1,0:T(8,128)(2,1)}, u32[]{:S(2)}) copy-start(bf16[32,128]{1,0:T(8,128)(2,1)} %constant.9.clone.perm_ref) | copy-start | bytes 24580
  17.0 49.9 %copy-start.3 = (bf16[128,128]{1,0:T(8,128)(2,1)S(1)}, bf16[128,128]{1,0:T(8,128)(2,1)}, u32[]{:S(2)}) copy-start(bf16[128,128]{1,0:T(8,128)(2,1)} %constant.10.clone.perm_ref) | copy-start | bytes 98308
  17.0 56.0 %copy-start.1 = (bf16[10,80,192]{2,1,0:T(8,128)(2,1)S(1)}, bf16[10,80,192]{2,1,0:T(8,128)(2,1)}, u32[]{:S(2)}) copy-start(bf16[10,80,192]{2,1,0:T(8,128)(2,1)} %constant.11.clone.spread_ref) | copy-start | bytes 921604
  17.0 56.0 %copy-start.2 = (bf16[2,2,64,128]{3,2,1,0:T(8,128)(2,1)S(1)}, bf16[2,2,64,128]{3,2,1,0:T(8,128)(2,1)}, u32[]{:S(2)}) copy-start(bf16[2,2,64,128]{3,2,1,0:T(8,128)(2,1)} %param.23) | copy-start | bytes 196612
  61.3 7.5 %collective-permute-start.1 = (bf16[512,128]{1,0:T(8,128)(2,1)S(1)}, bf16[512,128]{1,0:T(8,128)(2,1)S(1)}, u32[]{:S(2)}, u32[]{:S(2)}) collective-permute-start(bf16[512,128]{1,0:T(8,128)(2,1)S(1)} %get-tuple-element.21), channel_id=1, source_target_pairs={{8,0},{16,8},{24,16},{9,1},{17,9},{25,17},{10,2},{18,10},{26,18},{... | collective-permute-start | bytes 393224 | tf_op jit(solution)/shard_map/ppermute | solution.py:300
  64.1 4.8 %collective-permute-start = (bf16[512,128]{1,0:T(8,128)(2,1)S(1)}, bf16[512,128]{1,0:T(8,128)(2,1)S(1)}, u32[]{:S(2)}, u32[]{:S(2)}) collective-permute-start(bf16[512,128]{1,0:T(8,128)(2,1)S(1)} %get-tuple-element.20), channel_id=1, source_target_pairs={{0,8},{8,16},{16,24},{1,9},{9,17},{17,25},{2,10},{10,18},{18,26},{... | collective-permute-start | bytes 393224 | tf_op jit(solution)/shard_map/ppermute | solution.py:300
  68.9 10.1 %collective-permute-start.2 = (bf16[320,128]{1,0:T(8,128)(2,1)S(1)}, bf16[320,128]{1,0:T(8,128)(2,1)S(1)}, u32[]{:S(2)}, u32[]{:S(2)}) collective-permute-start(bf16[320,128]{1,0:T(8,128)(2,1)S(1)} %pad_maximum_fusion), channel_id=1, source_target_pairs={{0,1},{1,2},{2,3},{3,4},{4,5},{5,6},{6,7},{8,9},{9,10},{10,11},{11... | collective-permute-start | bytes 245768 | tf_op jit(solution)/shard_map/ppermute | solution.py:310
  71.7 7.3 %collective-permute-start.3 = (bf16[320,128]{1,0:T(8,128)(2,1)S(1)}, bf16[320,128]{1,0:T(8,128)(2,1)S(1)}, u32[]{:S(2)}, u32[]{:S(2)}) collective-permute-start(bf16[320,128]{1,0:T(8,128)(2,1)S(1)} %pad_maximum_fusion.1), channel_id=1, source_target_pairs={{1,0},{2,1},{3,2},{4,3},{5,4},{6,5},{7,6},{9,8},{10,9},{11,10},{12... | collective-permute-start | bytes 245768 | tf_op jit(solution)/shard_map/ppermute | solution.py:310
  73.0 6.0 %copy-start = (bf16[2,2,256,512]{3,2,1,0:T(8,128)(2,1)S(1)}, bf16[2,2,256,512]{3,2,1,0:T(8,128)(2,1)}, u32[]{:S(2)}) copy-start(bf16[2,2,256,512]{3,2,1,0:T(8,128)(2,1)} %param.27) | copy-start | bytes 3145732

commit v2 on v0

--- a/solution.py
+++ b/solution.py
@@ -411,7 +411,7 @@
     inner_hbm, top_ref, bottom_ref, fl_ref, fr_ref, above_ref, below_ref, spread_ref, one_ref,
     down2_ref, two_hbm, down3_hbm, three_hbm, down4_hbm, four_hbm,
     out_ref,
-    inner_ref, ext1, ext2, x1, x2, d2, d3, d4, flat, stage,
+    inner_ref, ext1, ext2, x1, x2, d2, d3, d4, stage,
     two_ref, down3_ref, three_ref, down4_ref, four_ref, sems,
 ):
     copies = [
@@ -519,38 +519,43 @@
     copies[0].wait()
     for rp in range(2):
         for j in range(2):
-            total = None
-            for v2 in range(2):
-                taps = jnp.concatenate(
+            taps = [
+                jnp.concatenate(
                     [d2[2 * rp + r, 2 * j + v2 + v] for r in range(4) for v in range(3)], axis=1
                 )
-                level = relu(dot(taps, two_ref[...])).astype(BF16)
-                part = dot(level, down3_ref[v2])
-                total = part if total is None else total + part
+                for v2 in range(2)
+            ]
+            level = relu(dot(jnp.concatenate(taps, axis=0), two_ref[...])).astype(BF16)
+            total = dot(level[:POINTS], down3_ref[0]) + dot(level[POINTS:], down3_ref[1])
             put(d3, rp, j, relu(total) * mask2, 1)
 
     copies[1].wait()
     copies[2].wait()
     total = None
     for i in range(2):
+        taps = [
+            jnp.concatenate([d3[i + u, j + v] for u in range(3) for v in range(3)], axis=1)
+            for j in range(2)
+        ]
+        level = relu(dot(jnp.concatenate(taps, axis=0), three_ref[...])).astype(BF16)
         for j in range(2):
-            taps = jnp.concatenate(
-                [d3[i + u, j + v] for u in range(3) for v in range(3)], axis=1
-            )
-            level = relu(dot(taps, three_ref[...])).astype(BF16)
-            part = dot(level, down4_ref[i * 2 + j])
+            part = dot(level[j * POINTS:(j + 1) * POINTS], down4_ref[i * 2 + j])
             total = part if total is None else total + part
-    put(d4, 0, 0, relu(total) * mask4, 0)
+    value = relu(total) * mask4
+
+    for p in range(4):
+        lanes = slice(p * 128, (p + 1) * 128)
+        stage[0, p, MARGIN:MARGIN + POINTS] = value[:, lanes]
+        for w in range(NWIN):
+            for u in range(3):
+                for v in range(3):
+                    start = MARGIN + (w + HALO + u - 1) * WIDE + HALO + v - 1
+                    tap = stage[0, p, start:start + SPOTS]
+                    d4[u, v, w * SPOTS:(w + 1) * SPOTS, lanes] = tap.astype(BF16)
 
     copies[3].wait()
-    first, count = HALO * WIDE, NWIN * WIDE
-    taps = jnp.concatenate(
-        [d4[u, v, first:first + count] for u in range(3) for v in range(3)], axis=1
-    )
-    flat[...] = relu(dot(taps, four_ref[...]))
-    for w in range(NWIN):
-        start = w * WIDE + HALO
-        out_ref[w] = flat[start:start + SPOTS].astype(BF16)
+    taps = jnp.concatenate([d4[u, v] for u in range(3) for v in range(3)], axis=1)
+    out_ref[...] = relu(dot(taps, four_ref[...])).astype(BF16)
 
 
 def encoder(inner, edges, spread, one, down2, two, down3, three, down4, four):
@@ -561,7 +566,7 @@
         encoder_kernel,
         in_specs=[hbm] + [vmem] * 9 + [hbm] * 5,
         out_specs=vmem,
-        out_shape=jax.ShapeDtypeStruct((NWIN, SPOTS, four.shape[-1]), BF16),
+        out_shape=jax.ShapeDtypeStruct((NWIN * SPOTS, four.shape[-1]), BF16),
         scratch_shapes=[
             pltpu.VMEM(inner.shape, BF16),
             pltpu.VMEM((2 * GROUP + 1, 160, 128), BF16),
@@ -570,8 +575,7 @@
             pltpu.VMEM((PHASES + 2, rim, 128), BF16),
             pltpu.VMEM((6, 6, POINTS, 128), BF16),
             pltpu.VMEM((4, 4, POINTS, 256), BF16),
-            pltpu.VMEM((3, 3, POINTS, 512), BF16),
-            pltpu.VMEM((NWIN * WIDE, 512), F32),
+            pltpu.VMEM((3, 3, NWIN * SPOTS, 512), BF16),
             pltpu.VMEM((2, 4, POINTS + 2 * MARGIN, 128), F32),
             pltpu.VMEM(two.shape, BF16),
             pltpu.VMEM(down3.shape, BF16),
@@ -631,7 +635,7 @@
         reduce_four.reshape(4, 256, 512),
         kernel_four.reshape(9 * 512, 512),
     )
-    return gridded, flat.transpose(2, 0, 1)
+    return gridded, flat.reshape(NWIN, SPOTS, -1).transpose(2, 0, 1)
 
 
 def solution(mesh):

time: 102 us -> 108 us (1.059)
  Pallas kernels: 39.9 us -> 45.5 us
    pallas_call x1, Pallas kernels: 21.7 us -> 27.3 us  [encoder(): pl.pallas_call(encoder_kernel, in_specs=[hbm] + [vmem] * 9 + [hbm] * 5, o...]
  transfers between devices with their start and end apart: 5 -> 5, of which waited for: 1 -> 1; matrix products, arithmetic and copies ran while one was open for 4% -> 4% of each run, Pallas kernels for 8% -> 7%
where the time goes in v2:
time: 108 us; the launch traced here: 106 us
  Pallas kernels  45.5 us (42%)
  waiting for transfers between devices  38.3 us (35%)
  starting transfers between devices  16.7 us (15%)
  local copies, waits for them, and re-layouts  3.01 us (3%)
  other arithmetic  1.14 us (1%)
  between operations  1.13 us (1%)
    all_to_all x1, waiting for transfers between devices, body(): lax.all_to_all(slots, axes, split_axis=0, concat_axis=0, tiled=True)  38.3 us
    pallas_call x1, Pallas kernels, encoder(): pl.pallas_call(encoder_kernel, in_specs=[hbm] + [vmem] * 9 + [hbm] * 5, o...  27.3 us
    all_to_all x1, starting transfers between devices, body(): lax.all_to_all(slots, axes, split_axis=0, concat_axis=0, tiled=True)  7.1 us
    pallas_call x1, Pallas kernels, resample(): pl.pallas_call(resample_kernel, in_specs=[smem, smem, smem, vmem, pl.Bloc...  6.1 us
    pallas_call x1, Pallas kernels, interior(): pl.pallas_call(interior_kernel, in_specs=[vmem] * 7, out_specs=vmem, out_...  5.92 us
    pallas_call x1, Pallas kernels, grid(): pl.pallas_call(grid_kernel, in_specs=[pl.BlockSpec(memory_space=pl.ANY),...  4.29 us
    ppermute x1, starting transfers between devices, exchange_columns(): lax.ppermute(right, 'tx', right_ward)  2.8 us
    ppermute x1, starting transfers between devices, exchange_rows(): lax.ppermute(last, 'ty', down_ward)  2.78 us
  transfers between devices with their start and end apart: 5, of which 1 were waited for; matrix products, arithmetic and copies ran while one was open for 4% of the time, Pallas kernels for 7%

profile of v2, /device:TPU:1, one launch (start us, length us, event | category | flops | bytes accessed | tf_op | source)
XLA Modules:
  0.0 105.8 jit_solution(16832072714990316223)
XLA Ops:
  0.6 6.1 %resample.1 = bf16[32,216,128]{2,1,0:T(8,128)(2,1)} custom-call(s32[64]{0:T(128)} %dest_ref.1, s32[64]{0:T(128)} %win_ref.1, s32[64]{0:T(128)} %choice_ref.1, bf16[128,64]{1,0:T(8,128)(2,1)} %bitcast.56, bf16[64,208,128]{2,1,0:T(8,128)(2,1)} %bitcast.45, bf16[8,128,128]{2,1,0:T(8,128)(2,1)} %bank_ref.1), custom_call_target="tpu_custom_call" | custom-call | tf_op jit(solution)/shard_map/resample/pallas_call | solution.py:119
  6.7 0.0 copy-start.7
  6.8 7.1 %all-to-all-start = ((bf16[32,216,128]{2,1,0:T(8,128)(2,1)}), bf16[32,216,128]{2,1,0:T(8,128)(2,1)S(1)}, u32[]{:S(2)}, u32[]{:S(2)}) async-start(bf16[32,216,128]{2,1,0:T(8,128)(2,1)} %resample.1), calls=%async_computation | async-start | bytes 3538944 | tf_op jit(solution)/shard_map/all_to_all | solution.py:619
  13.9 0.0 copy-start.6
  13.9 0.2 pad_bitcast_fusion
  14.2 0.7 copy.24
  14.9 0.7 copy.25
  15.6 1.3 %concatenate.12.one_ref = bf16[512,512]{1,0:T(8,128)(2,1)S(1)} concatenate(bf16[512,64]{1,0:T(8,128)(2,1)S(1)} %bitcast.47, bf16[512,64]{1,0:T(8,128)(2,1)S(1)} %bitcast.48, bf16[512,64]{1,0:T(8,128)(2,1)S(1)} %bitcast.49, bf16[512,64]{1,0:T(8,128)(2,1)S(1)} %bitcast.50, bf16[512,64]{1,0:T(8,128)(2,1)S(1)} %bitcast.51, bf16[512,64]{1,0:T(8,128)(2,1)S(1)} %bitcast.52, ...), dimensions={1} | concatenate | bytes 1048576 | tf_op jit(solution)/shard_map/concatenate | solution.py:601
  16.9 0.0 copy-start.4
  16.9 1.1 %fusion.2 = bf16[4,3,128,256]{3,2,1,0:T(8,128)(2,1)S(1)} fusion(bf16[3,3,128,128]{3,2,1,0:T(8,128)(2,1)} %param.24), kind=kLoop, calls=%fused_computation.4 | loop fusion | flops 3145728 | bytes 1081344 | tf_op jit(solution)/shard_map/concatenate | solution.py:607
  18.1 38.3 %all-to-all-done.got_hbm = bf16[32,216,128]{2,1,0:T(8,128)(2,1)S(1)} async-done(((bf16[32,216,128]{2,1,0:T(8,128)(2,1)}), bf16[32,216,128]{2,1,0:T(8,128)(2,1)S(1)}, u32[]{:S(2)}, u32[]{:S(2)}) %all-to-all-start) | async-done | bytes 1769504 | tf_op jit(solution)/shard_map/all_to_all | solution.py:619
  56.3 4.3 %grid.1 = (bf16[13,256,128]{2,1,0:T(8,128)(2,1)}, bf16[4096,128]{1,0:T(8,128)(2,1)S(1)}, bf16[512,128]{1,0:T(8,128)(2,1)S(1)}, bf16[512,128]{1,0:T(8,128)(2,1)S(1)}) custom-call(bf16[32,216,128]{2,1,0:T(8,128)(2,1)S(1)} %all-to-all-done.got_hbm, bf16[32,128]{1,0:T(8,128)(2,1)S(1)} %copy-done.5), custom_call_target="tpu_custom_call" | custom-call | tf_op jit(solution)/shard_map/grid/pallas_call | solution.py:229
  60.6 2.8 %collective-permute-start.1 = (bf16[512,128]{1,0:T(8,128)(2,1)S(1)}, bf16[512,128]{1,0:T(8,128)(2,1)S(1)}, u32[]{:S(2)}, u32[]{:S(2)}) collective-permute-start(bf16[512,128]{1,0:T(8,128)(2,1)S(1)} %get-tuple-element.20), channel_id=1, source_target_pairs={{8,0},{16,8},{24,16},{9,1},{17,9},{25,17},{10,2},{18,10},{26,18},{... | collective-permute-start | bytes 393224 | tf_op jit(solution)/shard_map/ppermute | solution.py:300
  63.4 2.8 %collective-permute-start = (bf16[512,128]{1,0:T(8,128)(2,1)S(1)}, bf16[512,128]{1,0:T(8,128)(2,1)S(1)}, u32[]{:S(2)}, u32[]{:S(2)}) collective-permute-start(bf16[512,128]{1,0:T(8,128)(2,1)S(1)} %get-tuple-element.19), channel_id=1, source_target_pairs={{0,8},{8,16},{16,24},{1,9},{9,17},{17,25},{2,10},{10,18},{18,26},{... | collective-permute-start | bytes 393224 | tf_op jit(solution)/shard_map/ppermute | solution.py:300
  66.2 1.9 %turn.1 = (bf16[4096,128]{1,0:T(8,128)(2,1)S(1)}, bf16[4096,128]{1,0:T(8,128)(2,1)S(1)}, bf16[384,128]{1,0:T(8,128)(2,1)S(1)}, bf16[256,128]{1,0:T(8,128)(2,1)S(1)}) custom-call(bf16[4096,128]{1,0:T(8,128)(2,1)S(1)} %get-tuple-element.16.lines_ref, bf16[128,128]{1,0:T(8,128)(2,1)S(1)} %copy-done.4), custom_call_target="tpu_custom_call" | custom-call | flops 268435456 | bytes 8388608 | tf_op jit(solution)/shard_map/turn/pallas_call | solution.py:278
  68.2 0.0 collective-permute-done.1.fr_ref
  68.2 0.0 collective-permute-done.fl_ref
  68.2 2.8 %collective-permute-start.2 = (bf16[320,128]{1,0:T(8,128)(2,1)S(1)}, bf16[320,128]{1,0:T(8,128)(2,1)S(1)}, u32[]{:S(2)}, u32[]{:S(2)}) collective-permute-start(bf16[320,128]{1,0:T(8,128)(2,1)S(1)} %pad_maximum_fusion), channel_id=1, source_target_pairs={{0,1},{1,2},{2,3},{3,4},{4,5},{5,6},{6,7},{8,9},{9,10},{10,11},{11... | collective-permute-start | bytes 245768 | tf_op jit(solution)/shard_map/ppermute | solution.py:310
  71.0 1.3 %collective-permute-start.3 = (bf16[320,128]{1,0:T(8,128)(2,1)S(1)}, bf16[320,128]{1,0:T(8,128)(2,1)S(1)}, u32[]{:S(2)}, u32[]{:S(2)}) collective-permute-start(bf16[320,128]{1,0:T(8,128)(2,1)S(1)} %pad_maximum_fusion.1), channel_id=1, source_target_pairs={{1,0},{2,1},{3,2},{4,3},{5,4},{6,5},{7,6},{9,8},{10,9},{11,10},{12... | collective-permute-start | bytes 245768 | tf_op jit(solution)/shard_map/ppermute | solution.py:310
  72.3 0.0 copy-start
  72.4 0.0 copy-start.1
  72.4 5.9 %interior.1.inner_hbm = bf16[4,4,560,128]{3,2,1,0:T(8,128)(2,1)S(1)} custom-call(bf16[4096,128]{1,0:T(8,128)(2,1)S(1)} %get-tuple-element.17.main_ref, bf16[4096,128]{1,0:T(8,128)(2,1)S(1)} %get-tuple-element.18.lower_ref, bf16[512,128]{1,0:T(8,128)(2,1)S(1)} %collective-permute-done.fl_ref, bf16[512,128]{1,0:T(8,128)(2,1)S(1)} %collective-permute-done.1.fr_ref, ...), custom_call_target="tpu_custom_call" | custom-call | flops 3523215360 | bytes 16777216 | tf_op jit(solution)/shard_map/interior/pallas_call | solution.py:390
  78.3 0.0 collective-permute-done.3.below_ref
  78.3 27.3 %encoder.1 = bf16[512,512]{1,0:T(8,128)(2,1)} custom-call(bf16[4,4,560,128]{3,2,1,0:T(8,128)(2,1)S(1)} %interior.1.inner_hbm, bf16[384,128]{1,0:T(8,128)(2,1)S(1)} %get-tuple-element.22.top_ref, bf16[256,128]{1,0:T(8,128)(2,1)S(1)} %get-tuple-element.23.bottom_ref, bf16[512,128]{1,0:T(8,128)(2,1)S(1)} %collective-permute-done.fl_ref, ...), custom_call_target="tpu_custom_call" | custom-call | tf_op jit(solution)/shard_map/encoder/pallas_call | solution.py:565
  (25 shorter events, 0.1 us)
Async XLA Ops:
  6.7 7.1 %copy-start.7 = (bf16[3,3,13,64]{3,2,1,0:T(8,128)(2,1)S(1)}, bf16[3,3,13,64]{3,2,1,0:T(8,128)(2,1)}, u32[]{:S(2)}) copy-start(bf16[3,3,13,64]{3,2,1,0:T(8,128)(2,1)} %param.22) | copy-start | bytes 44932
  6.8 49.6 %all-to-all-start = ((bf16[32,216,128]{2,1,0:T(8,128)(2,1)}), bf16[32,216,128]{2,1,0:T(8,128)(2,1)S(1)}, u32[]{:S(2)}, u32[]{:S(2)}) async-start(bf16[32,216,128]{2,1,0:T(8,128)(2,1)} %resample.1), calls=%async_computation | async-start | bytes 3538944 | tf_op jit(solution)/shard_map/all_to_all | solution.py:619
  13.9 1.7 %copy-start.6 = (bf16[2,2,128,256]{3,2,1,0:T(8,128)(2,1)S(1)}, bf16[2,2,128,256]{3,2,1,0:T(8,128)(2,1)}, u32[]{:S(2)}) copy-start(bf16[2,2,128,256]{3,2,1,0:T(8,128)(2,1)} %param.25) | copy-start | bytes 786436
  15.6 40.7 %copy-start.5 = (bf16[32,128]{1,0:T(8,128)(2,1)S(1)}, bf16[32,128]{1,0:T(8,128)(2,1)}, u32[]{:S(2)}) copy-start(bf16[32,128]{1,0:T(8,128)(2,1)} %constant.9.clone.perm_ref) | copy-start | bytes 24580
  16.9 49.3 %copy-start.4 = (bf16[128,128]{1,0:T(8,128)(2,1)S(1)}, bf16[128,128]{1,0:T(8,128)(2,1)}, u32[]{:S(2)}) copy-start(bf16[128,128]{1,0:T(8,128)(2,1)} %constant.10.clone.perm_ref) | copy-start | bytes 98308
  56.3 16.0 %copy-start.2 = (bf16[10,80,192]{2,1,0:T(8,128)(2,1)S(1)}, bf16[10,80,192]{2,1,0:T(8,128)(2,1)}, u32[]{:S(2)}) copy-start(bf16[10,80,192]{2,1,0:T(8,128)(2,1)} %constant.11.clone.spread_ref) | copy-start | bytes 921604
  56.3 16.0 %copy-start.3 = (bf16[2,2,64,128]{3,2,1,0:T(8,128)(2,1)S(1)}, bf16[2,2,64,128]{3,2,1,0:T(8,128)(2,1)}, u32[]{:S(2)}) copy-start(bf16[2,2,64,128]{3,2,1,0:T(8,128)(2,1)} %param.23) | copy-start | bytes 196612
  60.6 7.5 %collective-permute-start.1 = (bf16[512,128]{1,0:T(8,128)(2,1)S(1)}, bf16[512,128]{1,0:T(8,128)(2,1)S(1)}, u32[]{:S(2)}, u32[]{:S(2)}) collective-permute-start(bf16[512,128]{1,0:T(8,128)(2,1)S(1)} %get-tuple-element.20), channel_id=1, source_target_pairs={{8,0},{16,8},{24,16},{9,1},{17,9},{25,17},{10,2},{18,10},{26,18},{... | collective-permute-start | bytes 393224 | tf_op jit(solution)/shard_map/ppermute | solution.py:300
  63.4 4.8 %collective-permute-start = (bf16[512,128]{1,0:T(8,128)(2,1)S(1)}, bf16[512,128]{1,0:T(8,128)(2,1)S(1)}, u32[]{:S(2)}, u32[]{:S(2)}) collective-permute-start(bf16[512,128]{1,0:T(8,128)(2,1)S(1)} %get-tuple-element.19), channel_id=1, source_target_pairs={{0,8},{8,16},{16,24},{1,9},{9,17},{17,25},{2,10},{10,18},{18,26},{... | collective-permute-start | bytes 393224 | tf_op jit(solution)/shard_map/ppermute | solution.py:300
  68.2 10.1 %collective-permute-start.2 = (bf16[320,128]{1,0:T(8,128)(2,1)S(1)}, bf16[320,128]{1,0:T(8,128)(2,1)S(1)}, u32[]{:S(2)}, u32[]{:S(2)}) collective-permute-start(bf16[320,128]{1,0:T(8,128)(2,1)S(1)} %pad_maximum_fusion), channel_id=1, source_target_pairs={{0,1},{1,2},{2,3},{3,4},{4,5},{5,6},{6,7},{8,9},{9,10},{10,11},{11... | collective-permute-start | bytes 245768 | tf_op jit(solution)/shard_map/ppermute | solution.py:310
  71.0 7.3 %collective-permute-start.3 = (bf16[320,128]{1,0:T(8,128)(2,1)S(1)}, bf16[320,128]{1,0:T(8,128)(2,1)S(1)}, u32[]{:S(2)}, u32[]{:S(2)}) collective-permute-start(bf16[320,128]{1,0:T(8,128)(2,1)S(1)} %pad_maximum_fusion.1), channel_id=1, source_target_pairs={{1,0},{2,1},{3,2},{4,3},{5,4},{6,5},{7,6},{9,8},{10,9},{11,10},{12... | collective-permute-start | bytes 245768 | tf_op jit(solution)/shard_map/ppermute | solution.py:310
  72.3 6.0 %copy-start = (bf16[3,3,256,256]{3,2,1,0:T(8,128)(2,1)S(1)}, bf16[3,3,256,256]{3,2,1,0:T(8,128)(2,1)}, u32[]{:S(2)}) copy-start(bf16[3,3,256,256]{3,2,1,0:T(8,128)(2,1)} %param.26) | copy-start | bytes 3538948
  72.4 6.0 %copy-start.1 = (bf16[2,2,256,512]{3,2,1,0:T(8,128)(2,1)S(1)}, bf16[2,2,256,512]{3,2,1,0:T(8,128)(2,1)}, u32[]{:S(2)}) copy-start(bf16[2,2,256,512]{3,2,1,0:T(8,128)(2,1)} %param.27) | copy-start | bytes 3145732

commit v3 on v2

--- a/solution.py
+++ b/solution.py
@@ -334,6 +334,14 @@
     return jnp.maximum(x, 0.0)
 
 
+def summed(taps, weights_ref, depth):
+    total = None
+    for k, tap in enumerate(taps):
+        part = dot(tap(), weights_ref[k * depth:(k + 1) * depth])
+        total = part if total is None else total + part
+    return total
+
+
 def level_one(x1, x2, one_ref, down2_ref, store):
     for cb in range(4):
         for version, x in enumerate((x1, x2)):
@@ -519,27 +527,26 @@
     copies[0].wait()
     for rp in range(2):
         for j in range(2):
-            taps = [
-                jnp.concatenate(
-                    [d2[2 * rp + r, 2 * j + v2 + v] for r in range(4) for v in range(3)], axis=1
-                )
-                for v2 in range(2)
-            ]
-            level = relu(dot(jnp.concatenate(taps, axis=0), two_ref[...])).astype(BF16)
-            total = dot(level[:POINTS], down3_ref[0]) + dot(level[POINTS:], down3_ref[1])
+            total = None
+            for v2 in range(2):
+                spots = [(2 * rp + r, 2 * j + v2 + v) for r in range(4) for v in range(3)]
+                pairs = [
+                    lambda k=k: jnp.concatenate([d2[spots[2 * k]], d2[spots[2 * k + 1]]], axis=1)
+                    for k in range(6)
+                ]
+                level = relu(summed(pairs, two_ref, 256)).astype(BF16)
+                part = dot(level, down3_ref[v2])
+                total = part if total is None else total + part
             put(d3, rp, j, relu(total) * mask2, 1)
 
     copies[1].wait()
     copies[2].wait()
     total = None
     for i in range(2):
-        taps = [
-            jnp.concatenate([d3[i + u, j + v] for u in range(3) for v in range(3)], axis=1)
-            for j in range(2)
-        ]
-        level = relu(dot(jnp.concatenate(taps, axis=0), three_ref[...])).astype(BF16)
         for j in range(2):
-            part = dot(level[j * POINTS:(j + 1) * POINTS], down4_ref[i * 2 + j])
+            taps = [lambda u=u, v=v: d3[i + u, j + v] for u in range(3) for v in range(3)]
+            level = relu(summed(taps, three_ref, 256)).astype(BF16)
+            part = dot(level, down4_ref[i * 2 + j])
             total = part if total is None else total + part
     value = relu(total) * mask4
 
@@ -554,8 +561,8 @@
                     d4[u, v, w * SPOTS:(w + 1) * SPOTS, lanes] = tap.astype(BF16)
 
     copies[3].wait()
-    taps = jnp.concatenate([d4[u, v] for u in range(3) for v in range(3)], axis=1)
-    out_ref[...] = relu(dot(taps, four_ref[...])).astype(BF16)
+    taps = [lambda u=u, v=v: d4[u, v] for u in range(3) for v in range(3)]
+    out_ref[...] = relu(summed(taps, four_ref, 512)).astype(BF16)
 
 
 def encoder(inner, edges, spread, one, down2, two, down3, three, down4, four):

time: 108 us -> 101 us (0.935)
  Pallas kernels: 45.5 us -> 39.2 us
    pallas_call x1, Pallas kernels: 27.3 us -> 20.9 us  [encoder(): pl.pallas_call(encoder_kernel, in_specs=[hbm] + [vmem] * 9 + [hbm] * 5, o...]
  transfers between devices with their start and end apart: 5 -> 5, of which waited for: 1 -> 1; matrix products, arithmetic and copies ran while one was open for 4% -> 4% of each run, Pallas kernels for 7% -> 8%
where the time goes in v3:
time: 101 us; the launch traced here: 99.4 us
  Pallas kernels  39.2 us (39%)
  waiting for transfers between devices  38.3 us (38%)
  starting transfers between devices  16.7 us (17%)
  local copies, waits for them, and re-layouts  3.01 us (3%)
  other arithmetic  1.14 us (1%)
  between operations  1.11 us (1%)
    all_to_all x1, waiting for transfers between devices, body(): lax.all_to_all(slots, axes, split_axis=0, concat_axis=0, tiled=True)  38.3 us
    pallas_call x1, Pallas kernels, encoder(): pl.pallas_call(encoder_kernel, in_specs=[hbm] + [vmem] * 9 + [hbm] * 5, o...  20.9 us
    all_to_all x1, starting transfers between devices, body(): lax.all_to_all(slots, axes, split_axis=0, concat_axis=0, tiled=True)  7.1 us
    pallas_call x1, Pallas kernels, resample(): pl.pallas_call(resample_kernel, in_specs=[smem, smem, smem, vmem, pl.Bloc...  6.1 us
    pallas_call x1, Pallas kernels, interior(): pl.pallas_call(interior_kernel, in_specs=[vmem] * 7, out_specs=vmem, out_...  5.92 us
    pallas_call x1, Pallas kernels, grid(): pl.pallas_call(grid_kernel, in_specs=[pl.BlockSpec(memory_space=pl.ANY),...  4.29 us
    ppermute x1, starting transfers between devices, exchange_columns(): lax.ppermute(right, 'tx', right_ward)  2.8 us
    ppermute x1, starting transfers between devices, exchange_rows(): lax.ppermute(last, 'ty', down_ward)  2.78 us
  transfers between devices with their start and end apart: 5, of which 1 were waited for; matrix products, arithmetic and copies ran while one was open for 4% of the time, Pallas kernels for 8%

profile of v3, /device:TPU:1, one launch (start us, length us, event | category | flops | bytes accessed | tf_op | source)
XLA Modules:
  0.0 99.4 jit_solution(7819576162384051514)
XLA Ops:
  0.6 6.1 %resample.1 = bf16[32,216,128]{2,1,0:T(8,128)(2,1)} custom-call(s32[64]{0:T(128)} %dest_ref.1, s32[64]{0:T(128)} %win_ref.1, s32[64]{0:T(128)} %choice_ref.1, bf16[128,64]{1,0:T(8,128)(2,1)} %bitcast.56, bf16[64,208,128]{2,1,0:T(8,128)(2,1)} %bitcast.45, bf16[8,128,128]{2,1,0:T(8,128)(2,1)} %bank_ref.1), custom_call_target="tpu_custom_call" | custom-call | tf_op jit(solution)/shard_map/resample/pallas_call | solution.py:119
  6.7 0.0 copy-start.7
  6.8 7.1 %all-to-all-start = ((bf16[32,216,128]{2,1,0:T(8,128)(2,1)}), bf16[32,216,128]{2,1,0:T(8,128)(2,1)S(1)}, u32[]{:S(2)}, u32[]{:S(2)}) async-start(bf16[32,216,128]{2,1,0:T(8,128)(2,1)} %resample.1), calls=%async_computation | async-start | bytes 3538944 | tf_op jit(solution)/shard_map/all_to_all | solution.py:626
  13.9 0.0 copy-start.6
  13.9 0.2 pad_bitcast_fusion
  14.2 0.7 copy.24
  14.9 0.7 copy.25
  15.6 1.3 %concatenate.12.one_ref = bf16[512,512]{1,0:T(8,128)(2,1)S(1)} concatenate(bf16[512,64]{1,0:T(8,128)(2,1)S(1)} %bitcast.47, bf16[512,64]{1,0:T(8,128)(2,1)S(1)} %bitcast.48, bf16[512,64]{1,0:T(8,128)(2,1)S(1)} %bitcast.49, bf16[512,64]{1,0:T(8,128)(2,1)S(1)} %bitcast.50, bf16[512,64]{1,0:T(8,128)(2,1)S(1)} %bitcast.51, bf16[512,64]{1,0:T(8,128)(2,1)S(1)} %bitcast.52, ...), dimensions={1} | concatenate | bytes 1048576 | tf_op jit(solution)/shard_map/concatenate | solution.py:608
  16.9 0.0 copy-start.4
  16.9 1.1 %fusion.2 = bf16[4,3,128,256]{3,2,1,0:T(8,128)(2,1)S(1)} fusion(bf16[3,3,128,128]{3,2,1,0:T(8,128)(2,1)} %param.24), kind=kLoop, calls=%fused_computation.4 | loop fusion | flops 3145728 | bytes 1081344 | tf_op jit(solution)/shard_map/concatenate | solution.py:614
  18.1 38.3 %all-to-all-done.got_hbm = bf16[32,216,128]{2,1,0:T(8,128)(2,1)S(1)} async-done(((bf16[32,216,128]{2,1,0:T(8,128)(2,1)}), bf16[32,216,128]{2,1,0:T(8,128)(2,1)S(1)}, u32[]{:S(2)}, u32[]{:S(2)}) %all-to-all-start) | async-done | bytes 1769504 | tf_op jit(solution)/shard_map/all_to_all | solution.py:626
  56.3 4.3 %grid.1 = (bf16[13,256,128]{2,1,0:T(8,128)(2,1)}, bf16[4096,128]{1,0:T(8,128)(2,1)S(1)}, bf16[512,128]{1,0:T(8,128)(2,1)S(1)}, bf16[512,128]{1,0:T(8,128)(2,1)S(1)}) custom-call(bf16[32,216,128]{2,1,0:T(8,128)(2,1)S(1)} %all-to-all-done.got_hbm, bf16[32,128]{1,0:T(8,128)(2,1)S(1)} %copy-done.5), custom_call_target="tpu_custom_call" | custom-call | tf_op jit(solution)/shard_map/grid/pallas_call | solution.py:229
  60.6 2.8 %collective-permute-start.1 = (bf16[512,128]{1,0:T(8,128)(2,1)S(1)}, bf16[512,128]{1,0:T(8,128)(2,1)S(1)}, u32[]{:S(2)}, u32[]{:S(2)}) collective-permute-start(bf16[512,128]{1,0:T(8,128)(2,1)S(1)} %get-tuple-element.20), channel_id=1, source_target_pairs={{8,0},{16,8},{24,16},{9,1},{17,9},{25,17},{10,2},{18,10},{26,18},{... | collective-permute-start | bytes 393224 | tf_op jit(solution)/shard_map/ppermute | solution.py:300
  63.4 2.8 %collective-permute-start = (bf16[512,128]{1,0:T(8,128)(2,1)S(1)}, bf16[512,128]{1,0:T(8,128)(2,1)S(1)}, u32[]{:S(2)}, u32[]{:S(2)}) collective-permute-start(bf16[512,128]{1,0:T(8,128)(2,1)S(1)} %get-tuple-element.19), channel_id=1, source_target_pairs={{0,8},{8,16},{16,24},{1,9},{9,17},{17,25},{2,10},{10,18},{18,26},{... | collective-permute-start | bytes 393224 | tf_op jit(solution)/shard_map/ppermute | solution.py:300
  66.2 1.9 %turn.1 = (bf16[4096,128]{1,0:T(8,128)(2,1)S(1)}, bf16[4096,128]{1,0:T(8,128)(2,1)S(1)}, bf16[384,128]{1,0:T(8,128)(2,1)S(1)}, bf16[256,128]{1,0:T(8,128)(2,1)S(1)}) custom-call(bf16[4096,128]{1,0:T(8,128)(2,1)S(1)} %get-tuple-element.16.lines_ref, bf16[128,128]{1,0:T(8,128)(2,1)S(1)} %copy-done.4), custom_call_target="tpu_custom_call" | custom-call | flops 268435456 | bytes 8388608 | tf_op jit(solution)/shard_map/turn/pallas_call | solution.py:278
  68.2 0.0 collective-permute-done.1.fr_ref
  68.2 0.0 collective-permute-done.fl_ref
  68.2 2.8 %collective-permute-start.2 = (bf16[320,128]{1,0:T(8,128)(2,1)S(1)}, bf16[320,128]{1,0:T(8,128)(2,1)S(1)}, u32[]{:S(2)}, u32[]{:S(2)}) collective-permute-start(bf16[320,128]{1,0:T(8,128)(2,1)S(1)} %pad_maximum_fusion), channel_id=1, source_target_pairs={{0,1},{1,2},{2,3},{3,4},{4,5},{5,6},{6,7},{8,9},{9,10},{10,11},{11... | collective-permute-start | bytes 245768 | tf_op jit(solution)/shard_map/ppermute | solution.py:310
  71.0 1.3 %collective-permute-start.3 = (bf16[320,128]{1,0:T(8,128)(2,1)S(1)}, bf16[320,128]{1,0:T(8,128)(2,1)S(1)}, u32[]{:S(2)}, u32[]{:S(2)}) collective-permute-start(bf16[320,128]{1,0:T(8,128)(2,1)S(1)} %pad_maximum_fusion.1), channel_id=1, source_target_pairs={{1,0},{2,1},{3,2},{4,3},{5,4},{6,5},{7,6},{9,8},{10,9},{11,10},{12... | collective-permute-start | bytes 245768 | tf_op jit(solution)/shard_map/ppermute | solution.py:310
  72.3 0.0 copy-start
  72.4 0.0 copy-start.1
  72.4 5.9 %interior.1.inner_hbm = bf16[4,4,560,128]{3,2,1,0:T(8,128)(2,1)S(1)} custom-call(bf16[4096,128]{1,0:T(8,128)(2,1)S(1)} %get-tuple-element.17.main_ref, bf16[4096,128]{1,0:T(8,128)(2,1)S(1)} %get-tuple-element.18.lower_ref, bf16[512,128]{1,0:T(8,128)(2,1)S(1)} %collective-permute-done.fl_ref, bf16[512,128]{1,0:T(8,128)(2,1)S(1)} %collective-permute-done.1.fr_ref, ...), custom_call_target="tpu_custom_call" | custom-call | flops 3523215360 | bytes 16777216 | tf_op jit(solution)/shard_map/interior/pallas_call | solution.py:398
  78.3 0.0 collective-permute-done.3.below_ref
  78.3 20.9 %encoder.1 = bf16[512,512]{1,0:T(8,128)(2,1)} custom-call(bf16[4,4,560,128]{3,2,1,0:T(8,128)(2,1)S(1)} %interior.1.inner_hbm, bf16[384,128]{1,0:T(8,128)(2,1)S(1)} %get-tuple-element.22.top_ref, bf16[256,128]{1,0:T(8,128)(2,1)S(1)} %get-tuple-element.23.bottom_ref, bf16[512,128]{1,0:T(8,128)(2,1)S(1)} %collective-permute-done.fl_ref, ...), custom_call_target="tpu_custom_call" | custom-call | tf_op jit(solution)/shard_map/encoder/pallas_call | solution.py:572
  (25 shorter events, 0.1 us)
Async XLA Ops:
  6.7 7.1 %copy-start.7 = (bf16[3,3,13,64]{3,2,1,0:T(8,128)(2,1)S(1)}, bf16[3,3,13,64]{3,2,1,0:T(8,128)(2,1)}, u32[]{:S(2)}) copy-start(bf16[3,3,13,64]{3,2,1,0:T(8,128)(2,1)} %param.22) | copy-start | bytes 44932
  6.8 49.6 %all-to-all-start = ((bf16[32,216,128]{2,1,0:T(8,128)(2,1)}), bf16[32,216,128]{2,1,0:T(8,128)(2,1)S(1)}, u32[]{:S(2)}, u32[]{:S(2)}) async-start(bf16[32,216,128]{2,1,0:T(8,128)(2,1)} %resample.1), calls=%async_computation | async-start | bytes 3538944 | tf_op jit(solution)/shard_map/all_to_all | solution.py:626
  13.9 1.7 %copy-start.6 = (bf16[2,2,128,256]{3,2,1,0:T(8,128)(2,1)S(1)}, bf16[2,2,128,256]{3,2,1,0:T(8,128)(2,1)}, u32[]{:S(2)}) copy-start(bf16[2,2,128,256]{3,2,1,0:T(8,128)(2,1)} %param.25) | copy-start | bytes 786436
  15.6 40.7 %copy-start.5 = (bf16[32,128]{1,0:T(8,128)(2,1)S(1)}, bf16[32,128]{1,0:T(8,128)(2,1)}, u32[]{:S(2)}) copy-start(bf16[32,128]{1,0:T(8,128)(2,1)} %constant.9.clone.perm_ref) | copy-start | bytes 24580
  16.9 49.3 %copy-start.4 = (bf16[128,128]{1,0:T(8,128)(2,1)S(1)}, bf16[128,128]{1,0:T(8,128)(2,1)}, u32[]{:S(2)}) copy-start(bf16[128,128]{1,0:T(8,128)(2,1)} %constant.10.clone.perm_ref) | copy-start | bytes 98308
  56.3 16.0 %copy-start.2 = (bf16[10,80,192]{2,1,0:T(8,128)(2,1)S(1)}, bf16[10,80,192]{2,1,0:T(8,128)(2,1)}, u32[]{:S(2)}) copy-start(bf16[10,80,192]{2,1,0:T(8,128)(2,1)} %constant.11.clone.spread_ref) | copy-start | bytes 921604
  56.3 16.0 %copy-start.3 = (bf16[2,2,64,128]{3,2,1,0:T(8,128)(2,1)S(1)}, bf16[2,2,64,128]{3,2,1,0:T(8,128)(2,1)}, u32[]{:S(2)}) copy-start(bf16[2,2,64,128]{3,2,1,0:T(8,128)(2,1)} %param.23) | copy-start | bytes 196612
  60.6 7.5 %collective-permute-start.1 = (bf16[512,128]{1,0:T(8,128)(2,1)S(1)}, bf16[512,128]{1,0:T(8,128)(2,1)S(1)}, u32[]{:S(2)}, u32[]{:S(2)}) collective-permute-start(bf16[512,128]{1,0:T(8,128)(2,1)S(1)} %get-tuple-element.20), channel_id=1, source_target_pairs={{8,0},{16,8},{24,16},{9,1},{17,9},{25,17},{10,2},{18,10},{26,18},{... | collective-permute-start | bytes 393224 | tf_op jit(solution)/shard_map/ppermute | solution.py:300
  63.4 4.8 %collective-permute-start = (bf16[512,128]{1,0:T(8,128)(2,1)S(1)}, bf16[512,128]{1,0:T(8,128)(2,1)S(1)}, u32[]{:S(2)}, u32[]{:S(2)}) collective-permute-start(bf16[512,128]{1,0:T(8,128)(2,1)S(1)} %get-tuple-element.19), channel_id=1, source_target_pairs={{0,8},{8,16},{16,24},{1,9},{9,17},{17,25},{2,10},{10,18},{18,26},{... | collective-permute-start | bytes 393224 | tf_op jit(solution)/shard_map/ppermute | solution.py:300
  68.2 10.1 %collective-permute-start.2 = (bf16[320,128]{1,0:T(8,128)(2,1)S(1)}, bf16[320,128]{1,0:T(8,128)(2,1)S(1)}, u32[]{:S(2)}, u32[]{:S(2)}) collective-permute-start(bf16[320,128]{1,0:T(8,128)(2,1)S(1)} %pad_maximum_fusion), channel_id=1, source_target_pairs={{0,1},{1,2},{2,3},{3,4},{4,5},{5,6},{6,7},{8,9},{9,10},{10,11},{11... | collective-permute-start | bytes 245768 | tf_op jit(solution)/shard_map/ppermute | solution.py:310
  71.0 7.3 %collective-permute-start.3 = (bf16[320,128]{1,0:T(8,128)(2,1)S(1)}, bf16[320,128]{1,0:T(8,128)(2,1)S(1)}, u32[]{:S(2)}, u32[]{:S(2)}) collective-permute-start(bf16[320,128]{1,0:T(8,128)(2,1)S(1)} %pad_maximum_fusion.1), channel_id=1, source_target_pairs={{1,0},{2,1},{3,2},{4,3},{5,4},{6,5},{7,6},{9,8},{10,9},{11,10},{12... | collective-permute-start | bytes 245768 | tf_op jit(solution)/shard_map/ppermute | solution.py:310
  72.3 6.0 %copy-start = (bf16[3,3,256,256]{3,2,1,0:T(8,128)(2,1)S(1)}, bf16[3,3,256,256]{3,2,1,0:T(8,128)(2,1)}, u32[]{:S(2)}) copy-start(bf16[3,3,256,256]{3,2,1,0:T(8,128)(2,1)} %param.26) | copy-start | bytes 3538948
  72.4 6.0 %copy-start.1 = (bf16[2,2,256,512]{3,2,1,0:T(8,128)(2,1)S(1)}, bf16[2,2,256,512]{3,2,1,0:T(8,128)(2,1)}, u32[]{:S(2)}) copy-start(bf16[2,2,256,512]{3,2,1,0:T(8,128)(2,1)} %param.27) | copy-start | bytes 3145732

commit v4 on v3

--- a/solution.py
+++ b/solution.py
@@ -419,7 +419,7 @@
     inner_hbm, top_ref, bottom_ref, fl_ref, fr_ref, above_ref, below_ref, spread_ref, one_ref,
     down2_ref, two_hbm, down3_hbm, three_hbm, down4_hbm, four_hbm,
     out_ref,
-    inner_ref, ext1, ext2, x1, x2, d2, d3, d4, stage,
+    inner_ref, ext1, ext2, x1, x2, d2, d3, d4, stage, total_ref,
     two_ref, down3_ref, three_ref, down4_ref, four_ref, sems,
 ):
     copies = [
@@ -527,38 +527,49 @@
     copies[0].wait()
     for rp in range(2):
         for j in range(2):
-            total = None
-            for v2 in range(2):
+            total_ref[:, 0:256] = jnp.zeros((POINTS, 256), F32)
+
+            def column(v2, carry, rp=rp, j=j):
                 spots = [(2 * rp + r, 2 * j + v2 + v) for r in range(4) for v in range(3)]
                 pairs = [
                     lambda k=k: jnp.concatenate([d2[spots[2 * k]], d2[spots[2 * k + 1]]], axis=1)
                     for k in range(6)
                 ]
                 level = relu(summed(pairs, two_ref, 256)).astype(BF16)
-                part = dot(level, down3_ref[v2])
-                total = part if total is None else total + part
-            put(d3, rp, j, relu(total) * mask2, 1)
+                total_ref[:, 0:256] += dot(level, down3_ref[v2])
+                return carry
+
+            lax.fori_loop(0, 2, column, 0)
+            put(d3, rp, j, relu(total_ref[:, 0:256]) * mask2, 1)
 
     copies[1].wait()
     copies[2].wait()
-    total = None
-    for i in range(2):
-        for j in range(2):
-            taps = [lambda u=u, v=v: d3[i + u, j + v] for u in range(3) for v in range(3)]
-            level = relu(summed(taps, three_ref, 256)).astype(BF16)
-            part = dot(level, down4_ref[i * 2 + j])
-            total = part if total is None else total + part
-    value = relu(total) * mask4
+    total_ref[...] = jnp.zeros(total_ref.shape, F32)
+
+    def phase(t, carry):
+        i, j = t >> 1, t & 1
+        taps = [lambda u=u, v=v: d3[i + u, j + v] for u in range(3) for v in range(3)]
+        level = relu(summed(taps, three_ref, 256)).astype(BF16)
+        total_ref[...] += dot(level, down4_ref[t])
+        return carry
+
+    lax.fori_loop(0, 4, phase, 0)
+    value = relu(total_ref[...]) * mask4
 
     for p in range(4):
-        lanes = slice(p * 128, (p + 1) * 128)
-        stage[0, p, MARGIN:MARGIN + POINTS] = value[:, lanes]
+        stage[0, p, MARGIN:MARGIN + POINTS] = value[:, p * 128:(p + 1) * 128]
+
+    def pack(p, carry):
+        lanes = pl.ds(pl.multiple_of(p * 128, 128), 128)
         for w in range(NWIN):
             for u in range(3):
                 for v in range(3):
                     start = MARGIN + (w + HALO + u - 1) * WIDE + HALO + v - 1
                     tap = stage[0, p, start:start + SPOTS]
                     d4[u, v, w * SPOTS:(w + 1) * SPOTS, lanes] = tap.astype(BF16)
+        return carry
+
+    lax.fori_loop(0, 4, pack, 0)
 
     copies[3].wait()
     taps = [lambda u=u, v=v: d4[u, v] for u in range(3) for v in range(3)]
@@ -584,6 +595,7 @@
             pltpu.VMEM((4, 4, POINTS, 256), BF16),
             pltpu.VMEM((3, 3, NWIN * SPOTS, 512), BF16),
             pltpu.VMEM((2, 4, POINTS + 2 * MARGIN, 128), F32),
+            pltpu.VMEM((POINTS, 512), F32),
             pltpu.VMEM(two.shape, BF16),
             pltpu.VMEM(down3.shape, BF16),
             pltpu.VMEM(three.shape, BF16),

time: 101 us -> 104 us (1.030)
  Pallas kernels: 39.2 us -> 41.9 us
    pallas_call x1, Pallas kernels: 20.9 us -> 23.6 us  [encoder(): pl.pallas_call(encoder_kernel, in_specs=[hbm] + [vmem] * 9 + [hbm] * 5, o...]
where the time goes in v4:
time: 104 us; the launch traced here: 102 us
  Pallas kernels  41.9 us (40%)
  waiting for transfers between devices  38.3 us (37%)
  starting transfers between devices  16.9 us (16%)
  local copies, waits for them, and re-layouts  3.01 us (3%)
  other arithmetic  1.14 us (1%)
  between operations  1.11 us (1%)
    all_to_all x1, waiting for transfers between devices, body(): lax.all_to_all(slots, axes, split_axis=0, concat_axis=0, tiled=True)  38.3 us
    pallas_call x1, Pallas kernels, encoder(): pl.pallas_call(encoder_kernel, in_specs=[hbm] + [vmem] * 9 + [hbm] * 5, o...  23.6 us
    all_to_all x1, starting transfers between devices, body(): lax.all_to_all(slots, axes, split_axis=0, concat_axis=0, tiled=True)  7.1 us
    pallas_call x1, Pallas kernels, resample(): pl.pallas_call(resample_kernel, in_specs=[smem, smem, smem, vmem, pl.Bloc...  6.1 us
    pallas_call x1, Pallas kernels, interior(): pl.pallas_call(interior_kernel, in_specs=[vmem] * 7, out_specs=vmem, out_...  5.92 us
    pallas_call x1, Pallas kernels, grid(): pl.pallas_call(grid_kernel, in_specs=[pl.BlockSpec(memory_space=pl.ANY),...  4.29 us
    ppermute x1, starting transfers between devices, exchange_columns(): lax.ppermute(right, 'tx', right_ward)  2.8 us
    ppermute x1, starting transfers between devices, exchange_rows(): lax.ppermute(last, 'ty', down_ward)  2.78 us
  transfers between devices with their start and end apart: 5, of which 1 were waited for; matrix products, arithmetic and copies ran while one was open for 4% of the time, Pallas kernels for 8%

profile of v4, /device:TPU:1, one launch (start us, length us, event | category | flops | bytes accessed | tf_op | source)
XLA Modules:
  0.0 102.3 jit_solution(7029227865262132159)
XLA Ops:
  0.6 6.1 %resample.1 = bf16[32,216,128]{2,1,0:T(8,128)(2,1)} custom-call(s32[64]{0:T(128)} %dest_ref.1, s32[64]{0:T(128)} %win_ref.1, s32[64]{0:T(128)} %choice_ref.1, bf16[128,64]{1,0:T(8,128)(2,1)} %bitcast.56, bf16[64,208,128]{2,1,0:T(8,128)(2,1)} %bitcast.45, bf16[8,128,128]{2,1,0:T(8,128)(2,1)} %bank_ref.1), custom_call_target="tpu_custom_call" | custom-call | tf_op jit(solution)/shard_map/resample/pallas_call | solution.py:119
  6.7 0.0 copy-start.7
  6.8 7.1 %all-to-all-start = ((bf16[32,216,128]{2,1,0:T(8,128)(2,1)}), bf16[32,216,128]{2,1,0:T(8,128)(2,1)S(1)}, u32[]{:S(2)}, u32[]{:S(2)}) async-start(bf16[32,216,128]{2,1,0:T(8,128)(2,1)} %resample.1), calls=%async_computation | async-start | bytes 3538944 | tf_op jit(solution)/shard_map/all_to_all | solution.py:638
  13.9 0.0 copy-start.6
  13.9 0.2 pad_bitcast_fusion
  14.2 0.7 copy.24
  14.9 0.7 copy.25
  15.6 1.3 %concatenate.12.one_ref = bf16[512,512]{1,0:T(8,128)(2,1)S(1)} concatenate(bf16[512,64]{1,0:T(8,128)(2,1)S(1)} %bitcast.47, bf16[512,64]{1,0:T(8,128)(2,1)S(1)} %bitcast.48, bf16[512,64]{1,0:T(8,128)(2,1)S(1)} %bitcast.49, bf16[512,64]{1,0:T(8,128)(2,1)S(1)} %bitcast.50, bf16[512,64]{1,0:T(8,128)(2,1)S(1)} %bitcast.51, bf16[512,64]{1,0:T(8,128)(2,1)S(1)} %bitcast.52, ...), dimensions={1} | concatenate | bytes 1048576 | tf_op jit(solution)/shard_map/concatenate | solution.py:620
  16.9 0.0 copy-start.4
  16.9 1.1 %fusion.2 = bf16[4,3,128,256]{3,2,1,0:T(8,128)(2,1)S(1)} fusion(bf16[3,3,128,128]{3,2,1,0:T(8,128)(2,1)} %param.24), kind=kLoop, calls=%fused_computation.4 | loop fusion | flops 3145728 | bytes 1081344 | tf_op jit(solution)/shard_map/concatenate | solution.py:626
  18.1 38.3 %all-to-all-done.got_hbm = bf16[32,216,128]{2,1,0:T(8,128)(2,1)S(1)} async-done(((bf16[32,216,128]{2,1,0:T(8,128)(2,1)}), bf16[32,216,128]{2,1,0:T(8,128)(2,1)S(1)}, u32[]{:S(2)}, u32[]{:S(2)}) %all-to-all-start) | async-done | bytes 1769504 | tf_op jit(solution)/shard_map/all_to_all | solution.py:638
  56.3 4.3 %grid.1 = (bf16[13,256,128]{2,1,0:T(8,128)(2,1)}, bf16[4096,128]{1,0:T(8,128)(2,1)S(1)}, bf16[512,128]{1,0:T(8,128)(2,1)S(1)}, bf16[512,128]{1,0:T(8,128)(2,1)S(1)}) custom-call(bf16[32,216,128]{2,1,0:T(8,128)(2,1)S(1)} %all-to-all-done.got_hbm, bf16[32,128]{1,0:T(8,128)(2,1)S(1)} %copy-done.5), custom_call_target="tpu_custom_call" | custom-call | tf_op jit(solution)/shard_map/grid/pallas_call | solution.py:229
  60.6 2.8 %collective-permute-start.1 = (bf16[512,128]{1,0:T(8,128)(2,1)S(1)}, bf16[512,128]{1,0:T(8,128)(2,1)S(1)}, u32[]{:S(2)}, u32[]{:S(2)}) collective-permute-start(bf16[512,128]{1,0:T(8,128)(2,1)S(1)} %get-tuple-element.20), channel_id=1, source_target_pairs={{8,0},{16,8},{24,16},{9,1},{17,9},{25,17},{10,2},{18,10},{26,18},{... | collective-permute-start | bytes 393224 | tf_op jit(solution)/shard_map/ppermute | solution.py:300
  63.4 2.8 %collective-permute-start = (bf16[512,128]{1,0:T(8,128)(2,1)S(1)}, bf16[512,128]{1,0:T(8,128)(2,1)S(1)}, u32[]{:S(2)}, u32[]{:S(2)}) collective-permute-start(bf16[512,128]{1,0:T(8,128)(2,1)S(1)} %get-tuple-element.19), channel_id=1, source_target_pairs={{0,8},{8,16},{16,24},{1,9},{9,17},{17,25},{2,10},{10,18},{18,26},{... | collective-permute-start | bytes 393224 | tf_op jit(solution)/shard_map/ppermute | solution.py:300
  66.2 1.9 %turn.1 = (bf16[4096,128]{1,0:T(8,128)(2,1)S(1)}, bf16[4096,128]{1,0:T(8,128)(2,1)S(1)}, bf16[384,128]{1,0:T(8,128)(2,1)S(1)}, bf16[256,128]{1,0:T(8,128)(2,1)S(1)}) custom-call(bf16[4096,128]{1,0:T(8,128)(2,1)S(1)} %get-tuple-element.16.lines_ref, bf16[128,128]{1,0:T(8,128)(2,1)S(1)} %copy-done.4), custom_call_target="tpu_custom_call" | custom-call | flops 268435456 | bytes 8388608 | tf_op jit(solution)/shard_map/turn/pallas_call | solution.py:278
  68.2 0.0 collective-permute-done.1.fr_ref
  68.2 0.0 collective-permute-done.fl_ref
  68.2 2.8 %collective-permute-start.2 = (bf16[320,128]{1,0:T(8,128)(2,1)S(1)}, bf16[320,128]{1,0:T(8,128)(2,1)S(1)}, u32[]{:S(2)}, u32[]{:S(2)}) collective-permute-start(bf16[320,128]{1,0:T(8,128)(2,1)S(1)} %pad_maximum_fusion), channel_id=1, source_target_pairs={{0,1},{1,2},{2,3},{3,4},{4,5},{5,6},{6,7},{8,9},{9,10},{10,11},{11... | collective-permute-start | bytes 245768 | tf_op jit(solution)/shard_map/ppermute | solution.py:310
  71.0 1.5 %collective-permute-start.3 = (bf16[320,128]{1,0:T(8,128)(2,1)S(1)}, bf16[320,128]{1,0:T(8,128)(2,1)S(1)}, u32[]{:S(2)}, u32[]{:S(2)}) collective-permute-start(bf16[320,128]{1,0:T(8,128)(2,1)S(1)} %pad_maximum_fusion.1), channel_id=1, source_target_pairs={{1,0},{2,1},{3,2},{4,3},{5,4},{6,5},{7,6},{9,8},{10,9},{11,10},{12... | collective-permute-start | bytes 245768 | tf_op jit(solution)/shard_map/ppermute | solution.py:310
  72.5 0.0 copy-start
  72.5 0.0 copy-start.1
  72.6 5.9 %interior.1.inner_hbm = bf16[4,4,560,128]{3,2,1,0:T(8,128)(2,1)S(1)} custom-call(bf16[4096,128]{1,0:T(8,128)(2,1)S(1)} %get-tuple-element.17.main_ref, bf16[4096,128]{1,0:T(8,128)(2,1)S(1)} %get-tuple-element.18.lower_ref, bf16[512,128]{1,0:T(8,128)(2,1)S(1)} %collective-permute-done.fl_ref, bf16[512,128]{1,0:T(8,128)(2,1)S(1)} %collective-permute-done.1.fr_ref, ...), custom_call_target="tpu_custom_call" | custom-call | flops 3523215360 | bytes 16777216 | tf_op jit(solution)/shard_map/interior/pallas_call | solution.py:398
  78.5 0.0 collective-permute-done.3.below_ref
  78.5 23.6 %encoder.1 = bf16[512,512]{1,0:T(8,128)(2,1)} custom-call(bf16[4,4,560,128]{3,2,1,0:T(8,128)(2,1)S(1)} %interior.1.inner_hbm, bf16[384,128]{1,0:T(8,128)(2,1)S(1)} %get-tuple-element.22.top_ref, bf16[256,128]{1,0:T(8,128)(2,1)S(1)} %get-tuple-element.23.bottom_ref, bf16[512,128]{1,0:T(8,128)(2,1)S(1)} %collective-permute-done.fl_ref, ...), custom_call_target="tpu_custom_call" | custom-call | tf_op jit(solution)/shard_map/encoder/pallas_call | solution.py:583
  (25 shorter events, 0.1 us)
Async XLA Ops:
  6.7 7.1 %copy-start.7 = (bf16[3,3,13,64]{3,2,1,0:T(8,128)(2,1)S(1)}, bf16[3,3,13,64]{3,2,1,0:T(8,128)(2,1)}, u32[]{:S(2)}) copy-start(bf16[3,3,13,64]{3,2,1,0:T(8,128)(2,1)} %param.22) | copy-start | bytes 44932
  6.8 49.6 %all-to-all-start = ((bf16[32,216,128]{2,1,0:T(8,128)(2,1)}), bf16[32,216,128]{2,1,0:T(8,128)(2,1)S(1)}, u32[]{:S(2)}, u32[]{:S(2)}) async-start(bf16[32,216,128]{2,1,0:T(8,128)(2,1)} %resample.1), calls=%async_computation | async-start | bytes 3538944 | tf_op jit(solution)/shard_map/all_to_all | solution.py:638
  13.9 1.7 %copy-start.6 = (bf16[2,2,128,256]{3,2,1,0:T(8,128)(2,1)S(1)}, bf16[2,2,128,256]{3,2,1,0:T(8,128)(2,1)}, u32[]{:S(2)}) copy-start(bf16[2,2,128,256]{3,2,1,0:T(8,128)(2,1)} %param.25) | copy-start | bytes 786436
  15.6 40.7 %copy-start.5 = (bf16[32,128]{1,0:T(8,128)(2,1)S(1)}, bf16[32,128]{1,0:T(8,128)(2,1)}, u32[]{:S(2)}) copy-start(bf16[32,128]{1,0:T(8,128)(2,1)} %constant.9.clone.perm_ref) | copy-start | bytes 24580
  16.9 49.3 %copy-start.4 = (bf16[128,128]{1,0:T(8,128)(2,1)S(1)}, bf16[128,128]{1,0:T(8,128)(2,1)}, u32[]{:S(2)}) copy-start(bf16[128,128]{1,0:T(8,128)(2,1)} %constant.10.clone.perm_ref) | copy-start | bytes 98308
  56.3 16.2 %copy-start.2 = (bf16[10,80,192]{2,1,0:T(8,128)(2,1)S(1)}, bf16[10,80,192]{2,1,0:T(8,128)(2,1)}, u32[]{:S(2)}) copy-start(bf16[10,80,192]{2,1,0:T(8,128)(2,1)} %constant.11.clone.spread_ref) | copy-start | bytes 921604
  56.3 16.2 %copy-start.3 = (bf16[2,2,64,128]{3,2,1,0:T(8,128)(2,1)S(1)}, bf16[2,2,64,128]{3,2,1,0:T(8,128)(2,1)}, u32[]{:S(2)}) copy-start(bf16[2,2,64,128]{3,2,1,0:T(8,128)(2,1)} %param.23) | copy-start | bytes 196612
  60.6 7.5 %collective-permute-start.1 = (bf16[512,128]{1,0:T(8,128)(2,1)S(1)}, bf16[512,128]{1,0:T(8,128)(2,1)S(1)}, u32[]{:S(2)}, u32[]{:S(2)}) collective-permute-start(bf16[512,128]{1,0:T(8,128)(2,1)S(1)} %get-tuple-element.20), channel_id=1, source_target_pairs={{8,0},{16,8},{24,16},{9,1},{17,9},{25,17},{10,2},{18,10},{26,18},{... | collective-permute-start | bytes 393224 | tf_op jit(solution)/shard_map/ppermute | solution.py:300
  63.4 4.8 %collective-permute-start = (bf16[512,128]{1,0:T(8,128)(2,1)S(1)}, bf16[512,128]{1,0:T(8,128)(2,1)S(1)}, u32[]{:S(2)}, u32[]{:S(2)}) collective-permute-start(bf16[512,128]{1,0:T(8,128)(2,1)S(1)} %get-tuple-element.19), channel_id=1, source_target_pairs={{0,8},{8,16},{16,24},{1,9},{9,17},{17,25},{2,10},{10,18},{18,26},{... | collective-permute-start | bytes 393224 | tf_op jit(solution)/shard_map/ppermute | solution.py:300
  68.2 10.3 %collective-permute-start.2 = (bf16[320,128]{1,0:T(8,128)(2,1)S(1)}, bf16[320,128]{1,0:T(8,128)(2,1)S(1)}, u32[]{:S(2)}, u32[]{:S(2)}) collective-permute-start(bf16[320,128]{1,0:T(8,128)(2,1)S(1)} %pad_maximum_fusion), channel_id=1, source_target_pairs={{0,1},{1,2},{2,3},{3,4},{4,5},{5,6},{6,7},{8,9},{9,10},{10,11},{11... | collective-permute-start | bytes 245768 | tf_op jit(solution)/shard_map/ppermute | solution.py:310
  71.0 7.5 %collective-permute-start.3 = (bf16[320,128]{1,0:T(8,128)(2,1)S(1)}, bf16[320,128]{1,0:T(8,128)(2,1)S(1)}, u32[]{:S(2)}, u32[]{:S(2)}) collective-permute-start(bf16[320,128]{1,0:T(8,128)(2,1)S(1)} %pad_maximum_fusion.1), channel_id=1, source_target_pairs={{1,0},{2,1},{3,2},{4,3},{5,4},{6,5},{7,6},{9,8},{10,9},{11,10},{12... | collective-permute-start | bytes 245768 | tf_op jit(solution)/shard_map/ppermute | solution.py:310
  72.5 6.0 %copy-start = (bf16[3,3,256,256]{3,2,1,0:T(8,128)(2,1)S(1)}, bf16[3,3,256,256]{3,2,1,0:T(8,128)(2,1)}, u32[]{:S(2)}) copy-start(bf16[3,3,256,256]{3,2,1,0:T(8,128)(2,1)} %param.26) | copy-start | bytes 3538948
  72.5 6.0 %copy-start.1 = (bf16[2,2,256,512]{3,2,1,0:T(8,128)(2,1)S(1)}, bf16[2,2,256,512]{3,2,1,0:T(8,128)(2,1)}, u32[]{:S(2)}) copy-start(bf16[2,2,256,512]{3,2,1,0:T(8,128)(2,1)} %param.27) | copy-start | bytes 3145732

commit v5 on v3

--- a/solution.py
+++ b/solution.py
@@ -168,7 +168,8 @@
     lax.fori_loop(0, NWIN + 1, clear, 0)
     copy.wait()
 
-    def add(t, carry):
+    def add(piece, i, carry):
+        t = piece * size + i
         for k in range(CAP):
             w = win_ref[t, k]
             w = jnp.where(w < 0, NWIN, w)
@@ -179,7 +180,7 @@
 
     def add_piece(piece, carry):
         fetch(piece).wait()
-        return lax.fori_loop(piece * size, (piece + 1) * size, add, carry)
+        return lax.fori_loop(0, size, functools.partial(add, piece), carry, unroll=4)
 
     lax.fori_loop(0, PIECES, add_piece, 0)
 
@@ -334,10 +335,10 @@
     return jnp.maximum(x, 0.0)
 
 
-def summed(taps, weights_ref, depth):
+def summed(taps, weights_ref, depth, lanes=slice(None)):
     total = None
     for k, tap in enumerate(taps):
-        part = dot(tap(), weights_ref[k * depth:(k + 1) * depth])
+        part = dot(tap(), weights_ref[k * depth:(k + 1) * depth, lanes])
         total = part if total is None else total + part
     return total
 
@@ -489,7 +490,7 @@
     mask2 = jnp.concatenate([mask, mask], axis=1)
     mask4 = jnp.concatenate([mask2, mask2], axis=1)
 
-    def put(dst, i, j, value, last):
+    def put(dst, i, j, value, last, first=0):
         rows = [(i + 1, 0)]
         if i == last:
             rows.append((0, WIDE))
@@ -500,11 +501,12 @@
             cols.append((0, 1))
         if j == 0:
             cols.append((last + 2, -1))
-        dst[i + 1, j + 1] = value.astype(BF16)
+        height = value.shape[0]
+        dst[i + 1, j + 1, first:first + height] = value.astype(BF16)
         side = (i + j) % 2
         for p in range(value.shape[1] // 128):
             lanes = slice(p * 128, (p + 1) * 128)
-            stage[side, p, MARGIN:MARGIN + POINTS] = value[:, lanes]
+            stage[side, p, MARGIN + first:MARGIN + first + height] = value[:, lanes]
             for r, row_shift in rows:
                 for c, col_shift in cols:
                     shift = row_shift + col_shift
@@ -526,33 +528,36 @@
     copies[5].wait()
     copies[0].wait()
     for rp in range(2):
+        keep = slice(16, POINTS) if rp == 0 else slice(0, POINTS - 16)
         for j in range(2):
             total = None
             for v2 in range(2):
                 spots = [(2 * rp + r, 2 * j + v2 + v) for r in range(4) for v in range(3)]
                 pairs = [
-                    lambda k=k: jnp.concatenate([d2[spots[2 * k]], d2[spots[2 * k + 1]]], axis=1)
+                    lambda k=k: jnp.concatenate(
+                        [d2[(*spots[2 * k], keep)], d2[(*spots[2 * k + 1], keep)]], axis=1
+                    )
                     for k in range(6)
                 ]
                 level = relu(summed(pairs, two_ref, 256)).astype(BF16)
                 part = dot(level, down3_ref[v2])
                 total = part if total is None else total + part
-            put(d3, rp, j, relu(total) * mask2, 1)
+            put(d3, rp, j, relu(total) * mask2[keep], 1, keep.start)
 
     copies[1].wait()
     copies[2].wait()
-    total = None
+    total, keep = None, slice(16, POINTS - 16)
     for i in range(2):
         for j in range(2):
-            taps = [lambda u=u, v=v: d3[i + u, j + v] for u in range(3) for v in range(3)]
+            taps = [lambda u=u, v=v: d3[i + u, j + v, keep] for u in range(3) for v in range(3)]
             level = relu(summed(taps, three_ref, 256)).astype(BF16)
             part = dot(level, down4_ref[i * 2 + j])
             total = part if total is None else total + part
-    value = relu(total) * mask4
+    value = relu(total) * mask4[keep]
 
     for p in range(4):
         lanes = slice(p * 128, (p + 1) * 128)
-        stage[0, p, MARGIN:MARGIN + POINTS] = value[:, lanes]
+        stage[0, p, MARGIN + keep.start:MARGIN + keep.stop] = value[:, lanes]
         for w in range(NWIN):
             for u in range(3):
                 for v in range(3):
@@ -562,7 +567,9 @@
 
     copies[3].wait()
     taps = [lambda u=u, v=v: d4[u, v] for u in range(3) for v in range(3)]
-    out_ref[...] = relu(summed(taps, four_ref, 512)).astype(BF16)
+    for half in range(2):
+        lanes = slice(half * 256, (half + 1) * 256)
+        out_ref[:, lanes] = relu(summed(taps, four_ref, 512, lanes)).astype(BF16)
 
 
 def encoder(inner, edges, spread, one, down2, two, down3, three, down4, four):

time: 101 us -> 101 us (level)
  no operation moved by 1% of the time
where the time goes in v5:
time: 101 us; the launch traced here: 98.9 us
  Pallas kernels  38.6 us (38%)
  waiting for transfers between devices  38.3 us (38%)
  starting transfers between devices  16.7 us (17%)
  local copies, waits for them, and re-layouts  3.01 us (3%)
  other arithmetic  1.14 us (1%)
  between operations  1.11 us (1%)
    all_to_all x1, waiting for transfers between devices, body(): lax.all_to_all(slots, axes, split_axis=0, concat_axis=0, tiled=True)  38.3 us
    pallas_call x1, Pallas kernels, encoder(): pl.pallas_call(encoder_kernel, in_specs=[hbm] + [vmem] * 9 + [hbm] * 5, o...  20.6 us
    all_to_all x1, starting transfers between devices, body(): lax.all_to_all(slots, axes, split_axis=0, concat_axis=0, tiled=True)  7.1 us
    pallas_call x1, Pallas kernels, resample(): pl.pallas_call(resample_kernel, in_specs=[smem, smem, smem, vmem, pl.Bloc...  6.1 us
    pallas_call x1, Pallas kernels, interior(): pl.pallas_call(interior_kernel, in_specs=[vmem] * 7, out_specs=vmem, out_...  5.92 us
    pallas_call x1, Pallas kernels, grid(): pl.pallas_call(grid_kernel, in_specs=[pl.BlockSpec(memory_space=pl.ANY),...  4.15 us
    ppermute x1, starting transfers between devices, exchange_columns(): lax.ppermute(right, 'tx', right_ward)  2.8 us
    ppermute x1, starting transfers between devices, exchange_rows(): lax.ppermute(last, 'ty', down_ward)  2.78 us
  transfers between devices with their start and end apart: 5, of which 1 were waited for; matrix products, arithmetic and copies ran while one was open for 4% of the time, Pallas kernels for 8%

profile of v5, /device:TPU:1, one launch (start us, length us, event | category | flops | bytes accessed | tf_op | source)
XLA Modules:
  0.0 98.9 jit_solution(11696408340384894228)
XLA Ops:
  0.6 6.1 %resample.1 = bf16[32,216,128]{2,1,0:T(8,128)(2,1)} custom-call(s32[64]{0:T(128)} %dest_ref.1, s32[64]{0:T(128)} %win_ref.1, s32[64]{0:T(128)} %choice_ref.1, bf16[128,64]{1,0:T(8,128)(2,1)} %bitcast.56, bf16[64,208,128]{2,1,0:T(8,128)(2,1)} %bitcast.45, bf16[8,128,128]{2,1,0:T(8,128)(2,1)} %bank_ref.1), custom_call_target="tpu_custom_call" | custom-call | tf_op jit(solution)/shard_map/resample/pallas_call | solution.py:119
  6.7 0.0 copy-start.7
  6.8 7.1 %all-to-all-start = ((bf16[32,216,128]{2,1,0:T(8,128)(2,1)}), bf16[32,216,128]{2,1,0:T(8,128)(2,1)S(1)}, u32[]{:S(2)}, u32[]{:S(2)}) async-start(bf16[32,216,128]{2,1,0:T(8,128)(2,1)} %resample.1), calls=%async_computation | async-start | bytes 3538944 | tf_op jit(solution)/shard_map/all_to_all | solution.py:633
  13.9 0.0 copy-start.6
  13.9 0.2 pad_bitcast_fusion
  14.2 0.7 copy.24
  14.9 0.7 copy.25
  15.6 1.3 %concatenate.12.one_ref = bf16[512,512]{1,0:T(8,128)(2,1)S(1)} concatenate(bf16[512,64]{1,0:T(8,128)(2,1)S(1)} %bitcast.47, bf16[512,64]{1,0:T(8,128)(2,1)S(1)} %bitcast.48, bf16[512,64]{1,0:T(8,128)(2,1)S(1)} %bitcast.49, bf16[512,64]{1,0:T(8,128)(2,1)S(1)} %bitcast.50, bf16[512,64]{1,0:T(8,128)(2,1)S(1)} %bitcast.51, bf16[512,64]{1,0:T(8,128)(2,1)S(1)} %bitcast.52, ...), dimensions={1} | concatenate | bytes 1048576 | tf_op jit(solution)/shard_map/concatenate | solution.py:615
  16.9 0.0 copy-start.4
  16.9 1.1 %fusion.2 = bf16[4,3,128,256]{3,2,1,0:T(8,128)(2,1)S(1)} fusion(bf16[3,3,128,128]{3,2,1,0:T(8,128)(2,1)} %param.24), kind=kLoop, calls=%fused_computation.4 | loop fusion | flops 3145728 | bytes 1081344 | tf_op jit(solution)/shard_map/concatenate | solution.py:621
  18.1 38.3 %all-to-all-done.got_hbm = bf16[32,216,128]{2,1,0:T(8,128)(2,1)S(1)} async-done(((bf16[32,216,128]{2,1,0:T(8,128)(2,1)}), bf16[32,216,128]{2,1,0:T(8,128)(2,1)S(1)}, u32[]{:S(2)}, u32[]{:S(2)}) %all-to-all-start) | async-done | bytes 1769504 | tf_op jit(solution)/shard_map/all_to_all | solution.py:633
  56.3 4.1 %grid.1 = (bf16[13,256,128]{2,1,0:T(8,128)(2,1)}, bf16[4096,128]{1,0:T(8,128)(2,1)S(1)}, bf16[512,128]{1,0:T(8,128)(2,1)S(1)}, bf16[512,128]{1,0:T(8,128)(2,1)S(1)}) custom-call(bf16[32,216,128]{2,1,0:T(8,128)(2,1)S(1)} %all-to-all-done.got_hbm, bf16[32,128]{1,0:T(8,128)(2,1)S(1)} %copy-done.5), custom_call_target="tpu_custom_call" | custom-call | tf_op jit(solution)/shard_map/grid/pallas_call | solution.py:230
  60.5 2.8 %collective-permute-start.1 = (bf16[512,128]{1,0:T(8,128)(2,1)S(1)}, bf16[512,128]{1,0:T(8,128)(2,1)S(1)}, u32[]{:S(2)}, u32[]{:S(2)}) collective-permute-start(bf16[512,128]{1,0:T(8,128)(2,1)S(1)} %get-tuple-element.20), channel_id=1, source_target_pairs={{8,0},{16,8},{24,16},{9,1},{17,9},{25,17},{10,2},{18,10},{26,18},{... | collective-permute-start | bytes 393224 | tf_op jit(solution)/shard_map/ppermute | solution.py:301
  63.3 2.8 %collective-permute-start = (bf16[512,128]{1,0:T(8,128)(2,1)S(1)}, bf16[512,128]{1,0:T(8,128)(2,1)S(1)}, u32[]{:S(2)}, u32[]{:S(2)}) collective-permute-start(bf16[512,128]{1,0:T(8,128)(2,1)S(1)} %get-tuple-element.19), channel_id=1, source_target_pairs={{0,8},{8,16},{16,24},{1,9},{9,17},{17,25},{2,10},{10,18},{18,26},{... | collective-permute-start | bytes 393224 | tf_op jit(solution)/shard_map/ppermute | solution.py:301
  66.1 1.9 %turn.1 = (bf16[4096,128]{1,0:T(8,128)(2,1)S(1)}, bf16[4096,128]{1,0:T(8,128)(2,1)S(1)}, bf16[384,128]{1,0:T(8,128)(2,1)S(1)}, bf16[256,128]{1,0:T(8,128)(2,1)S(1)}) custom-call(bf16[4096,128]{1,0:T(8,128)(2,1)S(1)} %get-tuple-element.16.lines_ref, bf16[128,128]{1,0:T(8,128)(2,1)S(1)} %copy-done.4), custom_call_target="tpu_custom_call" | custom-call | flops 268435456 | bytes 8388608 | tf_op jit(solution)/shard_map/turn/pallas_call | solution.py:279
  68.0 0.0 collective-permute-done.1.fr_ref
  68.0 0.0 collective-permute-done.fl_ref
  68.1 2.8 %collective-permute-start.2 = (bf16[320,128]{1,0:T(8,128)(2,1)S(1)}, bf16[320,128]{1,0:T(8,128)(2,1)S(1)}, u32[]{:S(2)}, u32[]{:S(2)}) collective-permute-start(bf16[320,128]{1,0:T(8,128)(2,1)S(1)} %pad_maximum_fusion), channel_id=1, source_target_pairs={{0,1},{1,2},{2,3},{3,4},{4,5},{5,6},{6,7},{8,9},{9,10},{10,11},{11... | collective-permute-start | bytes 245768 | tf_op jit(solution)/shard_map/ppermute | solution.py:311
  70.9 1.3 %collective-permute-start.3 = (bf16[320,128]{1,0:T(8,128)(2,1)S(1)}, bf16[320,128]{1,0:T(8,128)(2,1)S(1)}, u32[]{:S(2)}, u32[]{:S(2)}) collective-permute-start(bf16[320,128]{1,0:T(8,128)(2,1)S(1)} %pad_maximum_fusion.1), channel_id=1, source_target_pairs={{1,0},{2,1},{3,2},{4,3},{5,4},{6,5},{7,6},{9,8},{10,9},{11,10},{12... | collective-permute-start | bytes 245768 | tf_op jit(solution)/shard_map/ppermute | solution.py:311
  72.2 0.0 copy-start
  72.2 0.0 copy-start.1
  72.2 5.9 %interior.1.inner_hbm = bf16[4,4,560,128]{3,2,1,0:T(8,128)(2,1)S(1)} custom-call(bf16[4096,128]{1,0:T(8,128)(2,1)S(1)} %get-tuple-element.17.main_ref, bf16[4096,128]{1,0:T(8,128)(2,1)S(1)} %get-tuple-element.18.lower_ref, bf16[512,128]{1,0:T(8,128)(2,1)S(1)} %collective-permute-done.fl_ref, bf16[512,128]{1,0:T(8,128)(2,1)S(1)} %collective-permute-done.1.fr_ref, ...), custom_call_target="tpu_custom_call" | custom-call | flops 3523215360 | bytes 16777216 | tf_op jit(solution)/shard_map/interior/pallas_call | solution.py:399
  78.2 0.0 collective-permute-done.2.above_ref
  78.2 20.6 %encoder.1 = bf16[512,512]{1,0:T(8,128)(2,1)} custom-call(bf16[4,4,560,128]{3,2,1,0:T(8,128)(2,1)S(1)} %interior.1.inner_hbm, bf16[384,128]{1,0:T(8,128)(2,1)S(1)} %get-tuple-element.22.top_ref, bf16[256,128]{1,0:T(8,128)(2,1)S(1)} %get-tuple-element.23.bottom_ref, bf16[512,128]{1,0:T(8,128)(2,1)S(1)} %collective-permute-done.fl_ref, ...), custom_call_target="tpu_custom_call" | custom-call | tf_op jit(solution)/shard_map/encoder/pallas_call | solution.py:579
  (25 shorter events, 0.1 us)
Async XLA Ops:
  6.7 7.1 %copy-start.7 = (bf16[3,3,13,64]{3,2,1,0:T(8,128)(2,1)S(1)}, bf16[3,3,13,64]{3,2,1,0:T(8,128)(2,1)}, u32[]{:S(2)}) copy-start(bf16[3,3,13,64]{3,2,1,0:T(8,128)(2,1)} %param.22) | copy-start | bytes 44932
  6.8 49.6 %all-to-all-start = ((bf16[32,216,128]{2,1,0:T(8,128)(2,1)}), bf16[32,216,128]{2,1,0:T(8,128)(2,1)S(1)}, u32[]{:S(2)}, u32[]{:S(2)}) async-start(bf16[32,216,128]{2,1,0:T(8,128)(2,1)} %resample.1), calls=%async_computation | async-start | bytes 3538944 | tf_op jit(solution)/shard_map/all_to_all | solution.py:633
  13.9 1.7 %copy-start.6 = (bf16[2,2,128,256]{3,2,1,0:T(8,128)(2,1)S(1)}, bf16[2,2,128,256]{3,2,1,0:T(8,128)(2,1)}, u32[]{:S(2)}) copy-start(bf16[2,2,128,256]{3,2,1,0:T(8,128)(2,1)} %param.25) | copy-start | bytes 786436
  15.6 40.7 %copy-start.5 = (bf16[32,128]{1,0:T(8,128)(2,1)S(1)}, bf16[32,128]{1,0:T(8,128)(2,1)}, u32[]{:S(2)}) copy-start(bf16[32,128]{1,0:T(8,128)(2,1)} %constant.9.clone.perm_ref) | copy-start | bytes 24580
  16.9 49.2 %copy-start.4 = (bf16[128,128]{1,0:T(8,128)(2,1)S(1)}, bf16[128,128]{1,0:T(8,128)(2,1)}, u32[]{:S(2)}) copy-start(bf16[128,128]{1,0:T(8,128)(2,1)} %constant.10.clone.perm_ref) | copy-start | bytes 98308
  56.3 15.9 %copy-start.2 = (bf16[10,80,192]{2,1,0:T(8,128)(2,1)S(1)}, bf16[10,80,192]{2,1,0:T(8,128)(2,1)}, u32[]{:S(2)}) copy-start(bf16[10,80,192]{2,1,0:T(8,128)(2,1)} %constant.11.clone.spread_ref) | copy-start | bytes 921604
  56.3 15.9 %copy-start.3 = (bf16[2,2,64,128]{3,2,1,0:T(8,128)(2,1)S(1)}, bf16[2,2,64,128]{3,2,1,0:T(8,128)(2,1)}, u32[]{:S(2)}) copy-start(bf16[2,2,64,128]{3,2,1,0:T(8,128)(2,1)} %param.23) | copy-start | bytes 196612
  60.5 7.5 %collective-permute-start.1 = (bf16[512,128]{1,0:T(8,128)(2,1)S(1)}, bf16[512,128]{1,0:T(8,128)(2,1)S(1)}, u32[]{:S(2)}, u32[]{:S(2)}) collective-permute-start(bf16[512,128]{1,0:T(8,128)(2,1)S(1)} %get-tuple-element.20), channel_id=1, source_target_pairs={{8,0},{16,8},{24,16},{9,1},{17,9},{25,17},{10,2},{18,10},{26,18},{... | collective-permute-start | bytes 393224 | tf_op jit(solution)/shard_map/ppermute | solution.py:301
  63.3 4.8 %collective-permute-start = (bf16[512,128]{1,0:T(8,128)(2,1)S(1)}, bf16[512,128]{1,0:T(8,128)(2,1)S(1)}, u32[]{:S(2)}, u32[]{:S(2)}) collective-permute-start(bf16[512,128]{1,0:T(8,128)(2,1)S(1)} %get-tuple-element.19), channel_id=1, source_target_pairs={{0,8},{8,16},{16,24},{1,9},{9,17},{17,25},{2,10},{10,18},{18,26},{... | collective-permute-start | bytes 393224 | tf_op jit(solution)/shard_map/ppermute | solution.py:301
  68.1 10.1 %collective-permute-start.2 = (bf16[320,128]{1,0:T(8,128)(2,1)S(1)}, bf16[320,128]{1,0:T(8,128)(2,1)S(1)}, u32[]{:S(2)}, u32[]{:S(2)}) collective-permute-start(bf16[320,128]{1,0:T(8,128)(2,1)S(1)} %pad_maximum_fusion), channel_id=1, source_target_pairs={{0,1},{1,2},{2,3},{3,4},{4,5},{5,6},{6,7},{8,9},{9,10},{10,11},{11... | collective-permute-start | bytes 245768 | tf_op jit(solution)/shard_map/ppermute | solution.py:311
  70.9 7.3 %collective-permute-start.3 = (bf16[320,128]{1,0:T(8,128)(2,1)S(1)}, bf16[320,128]{1,0:T(8,128)(2,1)S(1)}, u32[]{:S(2)}, u32[]{:S(2)}) collective-permute-start(bf16[320,128]{1,0:T(8,128)(2,1)S(1)} %pad_maximum_fusion.1), channel_id=1, source_target_pairs={{1,0},{2,1},{3,2},{4,3},{5,4},{6,5},{7,6},{9,8},{10,9},{11,10},{12... | collective-permute-start | bytes 245768 | tf_op jit(solution)/shard_map/ppermute | solution.py:311
  72.2 6.0 %copy-start = (bf16[3,3,256,256]{3,2,1,0:T(8,128)(2,1)S(1)}, bf16[3,3,256,256]{3,2,1,0:T(8,128)(2,1)}, u32[]{:S(2)}) copy-start(bf16[3,3,256,256]{3,2,1,0:T(8,128)(2,1)} %param.26) | copy-start | bytes 3538948
  72.2 6.0 %copy-start.1 = (bf16[2,2,256,512]{3,2,1,0:T(8,128)(2,1)S(1)}, bf16[2,2,256,512]{3,2,1,0:T(8,128)(2,1)}, u32[]{:S(2)}) copy-start(bf16[2,2,256,512]{3,2,1,0:T(8,128)(2,1)} %param.27) | copy-start | bytes 3145732

commit v6 on v5

--- a/solution.py
+++ b/solution.py
@@ -346,10 +346,14 @@
 def level_one(x1, x2, one_ref, down2_ref, store):
     for cb in range(4):
         for version, x in enumerate((x1, x2)):
-            taps = jnp.concatenate([x[2 * cb + k] for k in range(4)], axis=1)
-            level = relu(dot(taps, one_ref[...])).astype(BF16)
+            pairs = [
+                lambda k=k: jnp.concatenate([x[2 * cb + k], x[2 * cb + k + 1]], axis=1)
+                for k in (0, 2)
+            ]
             for half in range(2):
-                down = relu(dot(level[:, half * 256:(half + 1) * 256], down2_ref[...]))
+                lanes = slice(half * 256, (half + 1) * 256)
+                level = relu(summed(pairs, one_ref, 256, lanes)).astype(BF16)
+                down = relu(dot(level, down2_ref[...]))
                 store(2 * version + half, cb, down)
 
 

time: 101 us -> 105 us (1.040)
  Pallas kernels: 38.6 us -> 43 us
    pallas_call x1, Pallas kernels: 5.92 us -> 9.06 us  [interior(): pl.pallas_call(interior_kernel, in_specs=[vmem] * 7, out_specs=vmem, out_...]
    pallas_call x1, Pallas kernels: 20.6 us -> 21.8 us  [encoder(): pl.pallas_call(encoder_kernel, in_specs=[hbm] + [vmem] * 9 + [hbm] * 5, o...]
  transfers between devices with their start and end apart: 5 -> 5, of which waited for: 1 -> 1; matrix products, arithmetic and copies ran while one was open for 4% -> 4% of each run, Pallas kernels for 8% -> 11%
where the time goes in v6:
time: 105 us; the launch traced here: 103 us
  Pallas kernels  43 us (41%)
  waiting for transfers between devices  38.3 us (36%)
  starting transfers between devices  16.7 us (16%)
  local copies, waits for them, and re-layouts  3.01 us (3%)
  other arithmetic  1.14 us (1%)
  between operations  1.1 us (1%)
    all_to_all x1, waiting for transfers between devices, body(): lax.all_to_all(slots, axes, split_axis=0, concat_axis=0, tiled=True)  38.3 us
    pallas_call x1, Pallas kernels, encoder(): pl.pallas_call(encoder_kernel, in_specs=[hbm] + [vmem] * 9 + [hbm] * 5, o...  21.8 us
    pallas_call x1, Pallas kernels, interior(): pl.pallas_call(interior_kernel, in_specs=[vmem] * 7, out_specs=vmem, out_...  9.06 us
    all_to_all x1, starting transfers between devices, body(): lax.all_to_all(slots, axes, split_axis=0, concat_axis=0, tiled=True)  7.1 us
    pallas_call x1, Pallas kernels, resample(): pl.pallas_call(resample_kernel, in_specs=[smem, smem, smem, vmem, pl.Bloc...  6.1 us
    pallas_call x1, Pallas kernels, grid(): pl.pallas_call(grid_kernel, in_specs=[pl.BlockSpec(memory_space=pl.ANY),...  4.15 us
    ppermute x1, starting transfers between devices, exchange_columns(): lax.ppermute(right, 'tx', right_ward)  2.8 us
    ppermute x1, starting transfers between devices, exchange_rows(): lax.ppermute(last, 'ty', down_ward)  2.78 us
  transfers between devices with their start and end apart: 5, of which 1 were waited for; matrix products, arithmetic and copies ran while one was open for 4% of the time, Pallas kernels for 11%

profile of v6, /device:TPU:1, one launch (start us, length us, event | category | flops | bytes accessed | tf_op | source)
XLA Modules:
  0.0 103.3 jit_solution(12644437976625325922)
XLA Ops:
  0.6 6.1 %resample.1 = bf16[32,216,128]{2,1,0:T(8,128)(2,1)} custom-call(s32[64]{0:T(128)} %dest_ref.1, s32[64]{0:T(128)} %win_ref.1, s32[64]{0:T(128)} %choice_ref.1, bf16[128,64]{1,0:T(8,128)(2,1)} %bitcast.56, bf16[64,208,128]{2,1,0:T(8,128)(2,1)} %bitcast.45, bf16[8,128,128]{2,1,0:T(8,128)(2,1)} %bank_ref.1), custom_call_target="tpu_custom_call" | custom-call | tf_op jit(solution)/shard_map/resample/pallas_call | solution.py:119
  6.7 0.0 copy-start.7
  6.8 7.1 %all-to-all-start = ((bf16[32,216,128]{2,1,0:T(8,128)(2,1)}), bf16[32,216,128]{2,1,0:T(8,128)(2,1)S(1)}, u32[]{:S(2)}, u32[]{:S(2)}) async-start(bf16[32,216,128]{2,1,0:T(8,128)(2,1)} %resample.1), calls=%async_computation | async-start | bytes 3538944 | tf_op jit(solution)/shard_map/all_to_all | solution.py:637
  13.9 0.0 copy-start.6
  13.9 0.2 pad_bitcast_fusion
  14.2 0.7 copy.24
  14.9 0.7 copy.25
  15.6 1.3 %concatenate.12.one_ref = bf16[512,512]{1,0:T(8,128)(2,1)S(1)} concatenate(bf16[512,64]{1,0:T(8,128)(2,1)S(1)} %bitcast.47, bf16[512,64]{1,0:T(8,128)(2,1)S(1)} %bitcast.48, bf16[512,64]{1,0:T(8,128)(2,1)S(1)} %bitcast.49, bf16[512,64]{1,0:T(8,128)(2,1)S(1)} %bitcast.50, bf16[512,64]{1,0:T(8,128)(2,1)S(1)} %bitcast.51, bf16[512,64]{1,0:T(8,128)(2,1)S(1)} %bitcast.52, ...), dimensions={1} | concatenate | bytes 1048576 | tf_op jit(solution)/shard_map/concatenate | solution.py:619
  16.9 0.0 copy-start.4
  16.9 1.1 %fusion.2 = bf16[4,3,128,256]{3,2,1,0:T(8,128)(2,1)S(1)} fusion(bf16[3,3,128,128]{3,2,1,0:T(8,128)(2,1)} %param.24), kind=kLoop, calls=%fused_computation.4 | loop fusion | flops 3145728 | bytes 1081344 | tf_op jit(solution)/shard_map/concatenate | solution.py:625
  18.1 38.3 %all-to-all-done.got_hbm = bf16[32,216,128]{2,1,0:T(8,128)(2,1)S(1)} async-done(((bf16[32,216,128]{2,1,0:T(8,128)(2,1)}), bf16[32,216,128]{2,1,0:T(8,128)(2,1)S(1)}, u32[]{:S(2)}, u32[]{:S(2)}) %all-to-all-start) | async-done | bytes 1769504 | tf_op jit(solution)/shard_map/all_to_all | solution.py:637
  56.3 4.1 %grid.1 = (bf16[13,256,128]{2,1,0:T(8,128)(2,1)}, bf16[4096,128]{1,0:T(8,128)(2,1)S(1)}, bf16[512,128]{1,0:T(8,128)(2,1)S(1)}, bf16[512,128]{1,0:T(8,128)(2,1)S(1)}) custom-call(bf16[32,216,128]{2,1,0:T(8,128)(2,1)S(1)} %all-to-all-done.got_hbm, bf16[32,128]{1,0:T(8,128)(2,1)S(1)} %copy-done.5), custom_call_target="tpu_custom_call" | custom-call | tf_op jit(solution)/shard_map/grid/pallas_call | solution.py:230
  60.5 2.8 %collective-permute-start.1 = (bf16[512,128]{1,0:T(8,128)(2,1)S(1)}, bf16[512,128]{1,0:T(8,128)(2,1)S(1)}, u32[]{:S(2)}, u32[]{:S(2)}) collective-permute-start(bf16[512,128]{1,0:T(8,128)(2,1)S(1)} %get-tuple-element.20), channel_id=1, source_target_pairs={{8,0},{16,8},{24,16},{9,1},{17,9},{25,17},{10,2},{18,10},{26,18},{... | collective-permute-start | bytes 393224 | tf_op jit(solution)/shard_map/ppermute | solution.py:301
  63.3 2.8 %collective-permute-start = (bf16[512,128]{1,0:T(8,128)(2,1)S(1)}, bf16[512,128]{1,0:T(8,128)(2,1)S(1)}, u32[]{:S(2)}, u32[]{:S(2)}) collective-permute-start(bf16[512,128]{1,0:T(8,128)(2,1)S(1)} %get-tuple-element.19), channel_id=1, source_target_pairs={{0,8},{8,16},{16,24},{1,9},{9,17},{17,25},{2,10},{10,18},{18,26},{... | collective-permute-start | bytes 393224 | tf_op jit(solution)/shard_map/ppermute | solution.py:301
  66.1 1.9 %turn.1 = (bf16[4096,128]{1,0:T(8,128)(2,1)S(1)}, bf16[4096,128]{1,0:T(8,128)(2,1)S(1)}, bf16[384,128]{1,0:T(8,128)(2,1)S(1)}, bf16[256,128]{1,0:T(8,128)(2,1)S(1)}) custom-call(bf16[4096,128]{1,0:T(8,128)(2,1)S(1)} %get-tuple-element.16.lines_ref, bf16[128,128]{1,0:T(8,128)(2,1)S(1)} %copy-done.4), custom_call_target="tpu_custom_call" | custom-call | flops 268435456 | bytes 8388608 | tf_op jit(solution)/shard_map/turn/pallas_call | solution.py:279
  68.0 0.0 collective-permute-done.1.fr_ref
  68.0 0.0 collective-permute-done.fl_ref
  68.1 2.8 %collective-permute-start.2 = (bf16[320,128]{1,0:T(8,128)(2,1)S(1)}, bf16[320,128]{1,0:T(8,128)(2,1)S(1)}, u32[]{:S(2)}, u32[]{:S(2)}) collective-permute-start(bf16[320,128]{1,0:T(8,128)(2,1)S(1)} %pad_maximum_fusion), channel_id=1, source_target_pairs={{0,1},{1,2},{2,3},{3,4},{4,5},{5,6},{6,7},{8,9},{9,10},{10,11},{11... | collective-permute-start | bytes 245768 | tf_op jit(solution)/shard_map/ppermute | solution.py:311
  70.9 1.3 %collective-permute-start.3 = (bf16[320,128]{1,0:T(8,128)(2,1)S(1)}, bf16[320,128]{1,0:T(8,128)(2,1)S(1)}, u32[]{:S(2)}, u32[]{:S(2)}) collective-permute-start(bf16[320,128]{1,0:T(8,128)(2,1)S(1)} %pad_maximum_fusion.1), channel_id=1, source_target_pairs={{1,0},{2,1},{3,2},{4,3},{5,4},{6,5},{7,6},{9,8},{10,9},{11,10},{12... | collective-permute-start | bytes 245768 | tf_op jit(solution)/shard_map/ppermute | solution.py:311
  72.2 0.0 copy-start
  72.2 0.0 copy-start.1
  72.2 9.1 %interior.1.inner_hbm = bf16[4,4,560,128]{3,2,1,0:T(8,128)(2,1)S(1)} custom-call(bf16[4096,128]{1,0:T(8,128)(2,1)S(1)} %get-tuple-element.17.main_ref, bf16[4096,128]{1,0:T(8,128)(2,1)S(1)} %get-tuple-element.18.lower_ref, bf16[512,128]{1,0:T(8,128)(2,1)S(1)} %collective-permute-done.fl_ref, bf16[512,128]{1,0:T(8,128)(2,1)S(1)} %collective-permute-done.1.fr_ref, ...), custom_call_target="tpu_custom_call" | custom-call | flops 3523215360 | bytes 16777216 | tf_op jit(solution)/shard_map/interior/pallas_call | solution.py:403
  81.3 0.0 collective-permute-done.2.above_ref
  81.3 21.8 %encoder.1 = bf16[512,512]{1,0:T(8,128)(2,1)} custom-call(bf16[4,4,560,128]{3,2,1,0:T(8,128)(2,1)S(1)} %interior.1.inner_hbm, bf16[384,128]{1,0:T(8,128)(2,1)S(1)} %get-tuple-element.22.top_ref, bf16[256,128]{1,0:T(8,128)(2,1)S(1)} %get-tuple-element.23.bottom_ref, bf16[512,128]{1,0:T(8,128)(2,1)S(1)} %collective-permute-done.fl_ref, ...), custom_call_target="tpu_custom_call" | custom-call | tf_op jit(solution)/shard_map/encoder/pallas_call | solution.py:583
  (25 shorter events, 0.1 us)
Async XLA Ops:
  6.7 7.1 %copy-start.7 = (bf16[3,3,13,64]{3,2,1,0:T(8,128)(2,1)S(1)}, bf16[3,3,13,64]{3,2,1,0:T(8,128)(2,1)}, u32[]{:S(2)}) copy-start(bf16[3,3,13,64]{3,2,1,0:T(8,128)(2,1)} %param.22) | copy-start | bytes 44932
  6.8 49.6 %all-to-all-start = ((bf16[32,216,128]{2,1,0:T(8,128)(2,1)}), bf16[32,216,128]{2,1,0:T(8,128)(2,1)S(1)}, u32[]{:S(2)}, u32[]{:S(2)}) async-start(bf16[32,216,128]{2,1,0:T(8,128)(2,1)} %resample.1), calls=%async_computation | async-start | bytes 3538944 | tf_op jit(solution)/shard_map/all_to_all | solution.py:637
  13.9 1.7 %copy-start.6 = (bf16[2,2,128,256]{3,2,1,0:T(8,128)(2,1)S(1)}, bf16[2,2,128,256]{3,2,1,0:T(8,128)(2,1)}, u32[]{:S(2)}) copy-start(bf16[2,2,128,256]{3,2,1,0:T(8,128)(2,1)} %param.25) | copy-start | bytes 786436
  15.6 40.7 %copy-start.5 = (bf16[32,128]{1,0:T(8,128)(2,1)S(1)}, bf16[32,128]{1,0:T(8,128)(2,1)}, u32[]{:S(2)}) copy-start(bf16[32,128]{1,0:T(8,128)(2,1)} %constant.9.clone.perm_ref) | copy-start | bytes 24580
  16.9 49.2 %copy-start.4 = (bf16[128,128]{1,0:T(8,128)(2,1)S(1)}, bf16[128,128]{1,0:T(8,128)(2,1)}, u32[]{:S(2)}) copy-start(bf16[128,128]{1,0:T(8,128)(2,1)} %constant.10.clone.perm_ref) | copy-start | bytes 98308
  56.3 15.9 %copy-start.2 = (bf16[10,80,192]{2,1,0:T(8,128)(2,1)S(1)}, bf16[10,80,192]{2,1,0:T(8,128)(2,1)}, u32[]{:S(2)}) copy-start(bf16[10,80,192]{2,1,0:T(8,128)(2,1)} %constant.11.clone.spread_ref) | copy-start | bytes 921604
  56.3 15.9 %copy-start.3 = (bf16[2,2,64,128]{3,2,1,0:T(8,128)(2,1)S(1)}, bf16[2,2,64,128]{3,2,1,0:T(8,128)(2,1)}, u32[]{:S(2)}) copy-start(bf16[2,2,64,128]{3,2,1,0:T(8,128)(2,1)} %param.23) | copy-start | bytes 196612
  60.5 7.5 %collective-permute-start.1 = (bf16[512,128]{1,0:T(8,128)(2,1)S(1)}, bf16[512,128]{1,0:T(8,128)(2,1)S(1)}, u32[]{:S(2)}, u32[]{:S(2)}) collective-permute-start(bf16[512,128]{1,0:T(8,128)(2,1)S(1)} %get-tuple-element.20), channel_id=1, source_target_pairs={{8,0},{16,8},{24,16},{9,1},{17,9},{25,17},{10,2},{18,10},{26,18},{... | collective-permute-start | bytes 393224 | tf_op jit(solution)/shard_map/ppermute | solution.py:301
  63.3 4.8 %collective-permute-start = (bf16[512,128]{1,0:T(8,128)(2,1)S(1)}, bf16[512,128]{1,0:T(8,128)(2,1)S(1)}, u32[]{:S(2)}, u32[]{:S(2)}) collective-permute-start(bf16[512,128]{1,0:T(8,128)(2,1)S(1)} %get-tuple-element.19), channel_id=1, source_target_pairs={{0,8},{8,16},{16,24},{1,9},{9,17},{17,25},{2,10},{10,18},{18,26},{... | collective-permute-start | bytes 393224 | tf_op jit(solution)/shard_map/ppermute | solution.py:301
  68.1 13.2 %collective-permute-start.2 = (bf16[320,128]{1,0:T(8,128)(2,1)S(1)}, bf16[320,128]{1,0:T(8,128)(2,1)S(1)}, u32[]{:S(2)}, u32[]{:S(2)}) collective-permute-start(bf16[320,128]{1,0:T(8,128)(2,1)S(1)} %pad_maximum_fusion), channel_id=1, source_target_pairs={{0,1},{1,2},{2,3},{3,4},{4,5},{5,6},{6,7},{8,9},{9,10},{10,11},{11... | collective-permute-start | bytes 245768 | tf_op jit(solution)/shard_map/ppermute | solution.py:311
  70.9 10.4 %collective-permute-start.3 = (bf16[320,128]{1,0:T(8,128)(2,1)S(1)}, bf16[320,128]{1,0:T(8,128)(2,1)S(1)}, u32[]{:S(2)}, u32[]{:S(2)}) collective-permute-start(bf16[320,128]{1,0:T(8,128)(2,1)S(1)} %pad_maximum_fusion.1), channel_id=1, source_target_pairs={{1,0},{2,1},{3,2},{4,3},{5,4},{6,5},{7,6},{9,8},{10,9},{11,10},{12... | collective-permute-start | bytes 245768 | tf_op jit(solution)/shard_map/ppermute | solution.py:311
  72.2 9.1 %copy-start = (bf16[3,3,256,256]{3,2,1,0:T(8,128)(2,1)S(1)}, bf16[3,3,256,256]{3,2,1,0:T(8,128)(2,1)}, u32[]{:S(2)}) copy-start(bf16[3,3,256,256]{3,2,1,0:T(8,128)(2,1)} %param.26) | copy-start | bytes 3538948
  72.2 9.1 %copy-start.1 = (bf16[2,2,256,512]{3,2,1,0:T(8,128)(2,1)S(1)}, bf16[2,2,256,512]{3,2,1,0:T(8,128)(2,1)}, u32[]{:S(2)}) copy-start(bf16[2,2,256,512]{3,2,1,0:T(8,128)(2,1)} %param.27) | copy-start | bytes 3145732
